TPU v7x, 256 devices: a whole 4x4x8 slice. The times are simulated.
256 devices in a mesh: dp: 2 (over core), seq: 4 (over x), head: 32 (over z, y).
Axes of the slice: x: 4, y: 4, z: 8, core: 2. Of those that a mesh axis runs over, the one named last changes fastest.
Arguments:
- tokens_in: bfloat16 [32768, 3072], P(('dp', 'head'), 'seq'), parts along dimension 0, may hold values from -6 to 6
- qkv_weight: bfloat16 [3072, 3, 1536], P('head', None, 'seq'), may hold values from -0.109375 to 0.109375
- norm_gains: float32 [2, 128], replicated, may hold values from 0.1 to 1.9
- out_weight: bfloat16 [3072, 1536], P('seq', 'head'), may hold values from -0.15625 to 0.15625
- neighbours: int32 [256, 10], P(('dp', 'head')), parts along dimension 0, may hold values from -1 to 127, as said below
Outputs:
- attended: bfloat16 [32768, 3072], P(('dp', 'head'), 'seq'), parts along dimension 0
There are 2 independent parts, one for each index of `dp`. A program takes and returns all parts, laid end to end along the dimension named above; an argument that names none is the same for every part. Nothing has to cross between parts.
Inputs may be any that keep to these rules, and one draw needn't show every extreme that they name: `neighbours`: tiles are numbered in raster order over a clip of 32 x 2 x 2 tiles. Slot 0 of row t is t itself; the other slots name distinct tiles other than t that lie within one tile of t along each of the three dimensions, or -1, in no particular order.
All inputs are finite; a program needn't handle non-finite values.
Results may differ from a plain program's by a relative error of at most 0.008.
Values may be sent and summed in bfloat16 or wider, within the bound.
No kernel may reach another device: no remote copies, remote signals or barrier semaphores. Data moves between devices by JAX's collectives and lax.ppermute only.
A program may use at most 64 MiB of HBM per device.

v0:
```python
import functools
import math

import jax
import jax.numpy as jnp
from jax import lax
from jax.experimental import pallas as pl
from jax.experimental.pallas import tpu as pltpu
from jax.sharding import PartitionSpec as P

HD = 128
TILE = 128
FRAME = 4
NX, NY, NZ = 4, 4, 8
BF = jnp.bfloat16
F32 = jnp.float32
VMEM = pl.BlockSpec(memory_space=pltpu.VMEM)

SUB_0 = ((0, 0), (0, -1), (0, 1), (0, 2))
SUB_1 = ((0, 0), (-2, 0), (2, 0), (4, 0))
BUF_0 = ((0, 0), (-1, 0), (1, 0), (-2, 0), (2, 0), (-3, 0), (3, 0), (-4, 0))
BUF_1 = ((0, 0), (1, 0), (0, 1), (1, -1), (0, 2), (1, -2), (0, 3), (1, -3))
GROUPS = ((0, 1), (2,))


def moved(x, core0, core1):
    pairs = []
    for core, (dz, dy) in enumerate((core0, core1)):
        for z in range(NZ):
            for y in range(NY):
                target = ((z + dz) % NZ) * NY + (y + dy) % NY
                pairs.append((core * NZ * NY + z * NY + y, core * NZ * NY + target))
    return lax.ppermute(x, ("dp", "head"), pairs)


def frames_on(x, step):
    n = NZ * NY
    return lax.ppermute(x, "head", [(i, (i + step) % n) for i in range(n)])


def along(x, axis, step):
    n = lax.axis_size(axis)
    return lax.ppermute(x, axis, [(i, (i + step) % n) for i in range(n)])


def swapped(x):
    return lax.ppermute(x, "dp", [(0, 1), (1, 0)])


def halves_kernel(below, above, top, bottom):
    half = top.shape[0]
    top[...] = below[:half, :]
    bottom[...] = above[half:, :]


def halves(below, above):
    shape = jax.ShapeDtypeStruct((below.shape[0] // 2, below.shape[1]), BF)
    return call(halves_kernel, (shape, shape), (below, above), [], 2**34, 2**20, 8, "halves")


def gathered(tokens, mine):
    below = along(tokens, "seq", 1)
    above = along(tokens, "seq", -1)
    a = moved(mine, (0, 1), (2, 0))
    b = moved(mine, (0, -1), (-2, 0))
    c = moved(mine, (0, 2), (4, 0))
    s = jnp.concatenate([mine, a, b, c], axis=0)
    p1 = moved(s, (1, 0), (-1, 0))
    top, bottom = halves(below, above)
    below, above, top, bottom, p1, s = lax.optimization_barrier(
        (below, above, top, bottom, p1, s)
    )
    far_top = along(top, "seq", 1)
    far_bottom = along(bottom, "seq", -1)
    p3, p2 = moved(p1, (1, 0), (0, 1)), moved(s, (-1, 0), (0, -1))
    p5, p4 = moved(p3, (1, 0), (0, 1)), moved(p2, (-1, 0), (0, -1))
    pieces = (tokens, below, above, far_top, far_bottom)
    others = tuple(swapped(x) for x in pieces)
    *others, p5, p4 = lax.optimization_barrier((*others, p5, p4))
    p7, p6 = moved(p5, (1, 0), (0, 1)), moved(p4, (-1, 0), (0, -1))
    return pieces, others, (s, p1, p2, p3, p4, p5, p6, p7)


def prepare_kernel(columns, out_w, mine):
    core = lax.axis_index("dp")
    rows, cols = columns.shape[1:]
    half = rows // 2
    mine[:rows, :] = jnp.where(core == 0, columns[1], columns[2])
    mine[rows : rows + half, :] = jnp.where(core == 0, columns[0, :half, :], columns[0, half:, :])
    mine[rows + half :, :] = jnp.where(core == 0, out_w[:, :cols], out_w[:, cols:])


def place():
    head = lax.axis_index("head")
    return lax.axis_index("dp"), lax.axis_index("seq"), lax.div(head, NY), lax.rem(head, NY)


def block_of(z, y, core, k, i):
    z0, y0 = BUF_0[k][0] + SUB_0[i][0], BUF_0[k][1] + SUB_0[i][1]
    z1, y1 = BUF_1[k][0] + SUB_1[i][0], BUF_1[k][1] + SUB_1[i][1]
    dz = jnp.where(core == 0, z0 % NZ, z1 % NZ)
    dy = jnp.where(core == 0, y0 % NY, y1 % NY)
    return lax.rem(z + dz, NZ) * NY + lax.rem(y + dy, NY)


def normed(values, gain):
    mean_sq = jnp.mean(values * values, axis=-1, keepdims=True)
    return (values * lax.rsqrt(mean_sq + 1e-06) * gain).astype(BF)


def call(kernel, out_shape, args, scratch, flops, nbytes, limit, name):
    n = len(args)
    many = isinstance(out_shape, tuple)
    return pl.pallas_call(
        kernel,
        out_shape=out_shape,
        in_specs=[VMEM] * n,
        out_specs=(VMEM,) * len(out_shape) if many else VMEM,
        scratch_shapes=scratch,
        compiler_params=pltpu.CompilerParams(vmem_limit_bytes=limit * 2**20),
        cost_estimate=pl.CostEstimate(flops=flops, bytes_accessed=nbytes, transcendentals=0),
        name=name,
    )(*args)


def assemble(w, buffers, first, rows, core, z, y):
    size = buffers[0].shape[0] // 4
    for k, ref in enumerate(buffers):
        for i in range(4):
            at = pl.multiple_of(block_of(z, y, core, k, i) * rows, 16)
            start = i * size + first
            w[pl.ds(at, rows), :] = ref[start : start + rows, :]


def multiply_tokens(pieces, w, seq, store):
    own, below, above, far_top, far_bottom = pieces
    feats, half = own.shape[1], far_top.shape[0]

    def part(ref, step):
        at = pl.multiple_of(lax.rem(seq + step, NX) * feats, 128)
        return jnp.dot(ref[...], w[pl.ds(at, feats), :], preferred_element_type=F32)

    near = part(own, 0) + part(below, 3) + part(above, 1)
    store(slice(0, half), near[:half] + part(far_top, 2))
    store(slice(half, 2 * half), near[half:] + part(far_bottom, 2))


def kv_store(out, core, gains):
    def store(rows, product):
        for h in range(product.shape[1] // HD):
            at = slice(h * HD, (h + 1) * HD)
            part = product[:, at]
            out[rows, at] = jnp.where(core == 0, normed(part, gains[1:2, :]), part.astype(BF))

    return store


def cross_kernel(gains, *refs):
    pieces, buffers = refs[:5], refs[5:13]
    out, w = refs[13:]
    core, seq, z, y = place()
    rows = w.shape[0] // (NZ * NY)
    assemble(w, buffers, 0, rows, core, z, y)
    multiply_tokens(pieces, w, seq, kv_store(out, core, gains))


def same_kernel(gains, *refs):
    pieces, w, out = refs[:5], refs[5], refs[6]
    core, seq, _, _ = place()
    multiply_tokens(pieces, w, seq, kv_store(out, core, gains))


def pack_kernel(a, b, *outs):
    core = lax.axis_index("dp")
    for out, group in zip(outs, GROUPS, strict=True):
        at = slice(group[0] * HD, (group[-1] + 1) * HD)
        size = len(group) * HD
        out[:, :size] = jnp.where(core == 0, a[:, at], b[:, at])
        out[:, size:] = jnp.where(core == 0, b[:, at], a[:, at])


def project_kv(gains, tokens, others, buffers):
    rows, feats = tokens[0].shape
    depth, width = NX * feats, buffers[0].shape[1]
    part = jax.ShapeDtypeStruct((rows, width), BF)
    flops = 2 * rows * depth * width
    cross, w = call(
        cross_kernel, (part, jax.ShapeDtypeStruct((depth, width), BF)),
        (gains, *others, *buffers), [], flops, 6 * 2**20, 20, "project_cross",
    )
    cross = swapped(cross)
    same = call(same_kernel, part, (gains, *tokens, w), [], 8 * flops, 6 * 2**20, 20, "project_same")
    return call(
        pack_kernel,
        tuple(jax.ShapeDtypeStruct((rows, 2 * len(g) * HD), BF) for g in GROUPS),
        (same, cross), [], 0, 2**21, 8, "pack",
    )


def half_kernel(first, *refs):
    buffers, w = refs[:8], refs[8]
    core, _, z, y = place()
    assemble(w, buffers, first, w.shape[0] // (NZ * NY), core, z, y)


def half_of(buffers, first, rows, name):
    width = buffers[0].shape[1]
    shape = jax.ShapeDtypeStruct((NZ * NY * rows, width), BF)
    return call(
        functools.partial(half_kernel, first), shape, buffers, [], 0, 2**22, 8, name
    )


def attend_frame(scale, q, kv, keep, n):
    rows, keys = q.shape[0], kv.shape[0]
    at, size = n * HD, kv.shape[1] // 2
    score = lax.dot_general(
        q, kv[:, at : at + HD], (((1,), (1,)), ((), ())), preferred_element_type=F32
    )
    weight = jnp.exp2(score * scale).reshape(rows // TILE, TILE, keys)
    weight = jnp.where(keep[:, None, :] > 0, weight, 0.0).reshape(rows, keys).astype(BF)
    value = jnp.concatenate([kv[:, size + at : size + at + HD], jnp.ones((keys, HD), BF)], axis=1)
    return jnp.dot(weight, value, preferred_element_type=F32)


def kept(listed, frame, keys):
    tiles = listed.shape[0]
    lane = lax.div(lax.broadcasted_iota(jnp.int32, (tiles, keys), 1), TILE)
    tile = lane + frame * FRAME
    keep = jnp.zeros((tiles, keys), jnp.bool_)
    for s in range(listed.shape[1]):
        keep = keep | (tile == listed[:, s : s + 1])
    return jnp.where(keep & (tile >= 0), 1.0, 0.0)


def q_kernel(scale, gains, near, w_own, w_other, *refs):
    pieces, kvs = refs[:5], refs[5 : 5 + len(GROUPS)]
    q_ref, acc, w = refs[5 + len(GROUPS) :]
    core, seq, _, _ = place()
    rows = w.shape[0] // (2 * NZ * NY)
    for block in range(NZ * NY):
        span = slice(block * rows, (block + 1) * rows)
        a, b = w_own[span, :], w_other[span, :]
        at = 2 * block * rows
        w[at : at + rows, :] = jnp.where(core == 0, a, b)
        w[at + rows : at + 2 * rows, :] = jnp.where(core == 0, b, a)

    def store(span, product):
        for h in range(product.shape[1] // HD):
            at = slice(h * HD, (h + 1) * HD)
            q_ref[span, at] = normed(product[:, at], gains[0:1, :])

    multiply_tokens(pieces, w, seq, store)
    keep = kept(near[...], lax.axis_index("head"), q_ref.shape[0])
    for kv, group in zip(kvs, GROUPS, strict=True):
        for n, h in enumerate(group):
            acc[h] = attend_frame(scale, q_ref[:, h * HD : (h + 1) * HD], kv, keep, n)


def attend_kernel(scale, group, near, q_ref, acc, before, after, out):
    head = lax.axis_index("head")
    keep = [kept(near[...], head + step, q_ref.shape[0]) for step in (-1, 1)]
    for n, h in enumerate(group):
        q = q_ref[:, h * HD : (h + 1) * HD]
        total = acc[h] + attend_frame(scale, q, before, keep[0], n)
        total = total + attend_frame(scale, q, after, keep[1], n)
        out[:, n * HD : (n + 1) * HD] = (total[:, :HD] / total[:, HD:]).astype(BF)


def output_kernel(group, w_own, w_other, total, *refs):
    pieces, out = refs[:-1], refs[-1]
    core, seq = lax.axis_index("dp"), lax.axis_index("seq")
    width, cols = w_own.shape[0] // NX, w_own.shape[1]
    size = len(group) * HD
    for w, side in ((w_own, core), (w_other, 1 - core)):
        to = pl.ds(pl.multiple_of(side * cols, HD), cols)

        def part(ref, step, w=w):
            at = pl.multiple_of(lax.rem(seq + step, NX) * width + group[0] * HD, HD)
            return jnp.dot(ref[...], w[pl.ds(at, size), :], preferred_element_type=F32)

        near = part(pieces[0], 0) + part(pieces[1], 3) + part(pieces[2], 1)
        if total is not None:
            near = near + total[:, to]
        start = 0
        for far in pieces[3:]:
            rows = slice(start, start + far.shape[0])
            out[rows, to] = (near[rows] + part(far, 2)).astype(out.dtype)
            start += far.shape[0]


def first_kernel(group, w_own, w_other, *refs):
    output_kernel(group, w_own, w_other, None, *refs)


def ring_x(x):
    half = x.shape[0] // 2
    below = along(x, "seq", 1)
    above = along(x, "seq", -1)
    return x, below, above, along(below[:half], "seq", 1), along(above[half:], "seq", -1)


def direct_x(x):
    return x, along(x, "seq", 1), along(x, "seq", -1), along(x, "seq", 2)


def per_device(tokens_in, qkv_weight, norm_gains, out_weight, neighbours):
    rows, feats = tokens_in.shape
    width = qkv_weight.shape[2]
    heads = width // HD
    depth = qkv_weight.shape[0]
    mine = call(
        prepare_kernel,
        jax.ShapeDtypeStruct((depth * 3 // 2 + out_weight.shape[1], width), BF),
        (jnp.transpose(qkv_weight, (1, 0, 2)), jnp.transpose(out_weight)),
        [], 2**35, 2**20, 8, "prepare",
    )
    tokens, others, buffers = gathered(tokens_in, mine)

    kv = project_kv(norm_gains, tokens, others, buffers)
    sides = [[frames_on(x, step) for step in (1, -1)] for x in kv]
    scale = HD ** (-0.5) * math.log2(math.e)
    w_q = half_of(buffers, depth, depth // 2, "query_half")
    query, acc = call(
        functools.partial(q_kernel, scale),
        (
            jax.ShapeDtypeStruct((rows, width), BF),
            jax.ShapeDtypeStruct((heads, rows, 2 * HD), F32),
        ),
        (norm_gains, neighbours, w_q, swapped(w_q), *tokens, *kv),
        [pltpu.VMEM((NX * feats, width), BF)],
        2**35, 6 * 2**20, 20, "query",
    )
    first = depth * 3 // 2
    w_out = half_of(buffers, first, mine.shape[0] - first, "out_half")
    w_outs = (w_out, swapped(w_out))
    total = ()
    for g, group in enumerate(GROUPS):
        last = g == len(GROUPS) - 1
        out = call(
            functools.partial(attend_kernel, scale, group),
            jax.ShapeDtypeStruct((rows, len(group) * HD), BF),
            (neighbours, query, acc, *sides[g]),
            [], (2**35 if not last else 2**30), 4 * 2**20, 16, "attend_%d" % g,
        )
        pieces = (direct_x if last and g else ring_x)(out)
        total = (
            call(
                functools.partial(output_kernel if g else first_kernel, group),
                jax.ShapeDtypeStruct((rows, feats), BF if last else F32),
                (*w_outs, *total, *pieces),
                [], 8 * rows * feats * len(group) * HD, 5 * 2**20, 16, "output_%d" % g,
            ),
        )
    return total[0]


def solution(mesh):
    placed = (
        P(("dp", "head"), "seq"),
        P("head", None, "seq"),
        P(),
        P("seq", "head"),
        P(("dp", "head"), None),
    )
    return jax.shard_map(
        per_device, mesh=mesh, in_specs=placed, out_specs=P(("dp", "head"), "seq"), check_vma=False
    )
```

profile of v0, /device:TPU:1, one launch (start us, length us, event | category | flops | bytes accessed | tf_op | source)
XLA Modules:
  0.0 116.7 jit_solution(10648524916261114552)
XLA Ops:
  0.0 3.3 %collective-permute-start.1 = (bf16[512,768]{1,0:T(8,128)(2,1)}, bf16[512,768]{1,0:T(8,128)(2,1)S(1)}, u32[]{:S(2)}, u32[]{:S(2)}) collective-permute-start(bf16[512,768]{1,0:T(8,128)(2,1)} %refs_0_.3), channel_id=1, source_target_pairs={{0,96},{32,0},{64,32},{96,64},{1,97},{33,1},{65,33},{97,65},{2,98}... | collective-permute-start | bytes 2359304 | tf_op jit(solution)/shard_map/ppermute | solution.py:43
  5.2 7.0 %collective-permute-start.4 = (bf16[192,384]{1,0:T(8,128)(2,1)S(1)}, bf16[192,384]{1,0:T(8,128)(2,1)S(1)}, u32[]{:S(2)}, u32[]{:S(2)}) collective-permute-start(bf16[192,384]{1,0:T(8,128)(2,1)S(1)} %prepare.1), channel_id=1, source_target_pairs={{0,2},{1,3},{2,0},{3,1},{4,6},{5,7},{6,4},{7,5},{8,10},{9,11},{10,... | collective-permute-start | bytes 442376 | tf_op jit(solution)/shard_map/ppermute | solution.py:33
  12.2 2.4 %collective-permute-start.2 = (bf16[192,384]{1,0:T(8,128)(2,1)S(1)}, bf16[192,384]{1,0:T(8,128)(2,1)S(1)}, u32[]{:S(2)}, u32[]{:S(2)}) collective-permute-start(bf16[192,384]{1,0:T(8,128)(2,1)S(1)} %prepare.1), channel_id=1, source_target_pairs={{0,1},{1,2},{2,3},{3,0},{4,5},{5,6},{6,7},{7,4},{8,9},{9,10},{10,1... | collective-permute-start | bytes 442376 | tf_op jit(solution)/shard_map/ppermute | solution.py:33
  14.8 5.4 %collective-permute-done.3 = bf16[192,384]{1,0:T(8,128)(2,1)S(1)} collective-permute-done((bf16[192,384]{1,0:T(8,128)(2,1)S(1)}, bf16[192,384]{1,0:T(8,128)(2,1)S(1)}, u32[]{:S(2)}, u32[]{:S(2)}) %collective-permute-start.3) | collective-permute-done | bytes 147488 | tf_op jit(solution)/shard_map/ppermute | solution.py:33
  20.3 2.5 %collective-permute-start.5 = (bf16[768,384]{1,0:T(8,128)(2,1)S(1)}, bf16[768,384]{1,0:T(8,128)(2,1)S(1)}, u32[]{:S(2)}, u32[]{:S(2)}) collective-permute-start(bf16[768,384]{1,0:T(8,128)(2,1)S(1)} %pad_maximum_fusion.refs_0_.refs_5_), channel_id=1, source_target_pairs={{0,4},{1,5},{2,6},{3,7},{4,8},{5,9},{6,10},{7,11},{8,12},{9,13},{1... | collective-permute-start | bytes 1769480 | tf_op jit(solution)/shard_map/ppermute | solution.py:33
  22.9 6.7 %collective-permute-done.5.refs_1_.refs_6_ = bf16[768,384]{1,0:T(8,128)(2,1)S(1)} collective-permute-done((bf16[768,384]{1,0:T(8,128)(2,1)S(1)}, bf16[768,384]{1,0:T(8,128)(2,1)S(1)}, u32[]{:S(2)}, u32[]{:S(2)}) %collective-permute-start.5) | collective-permute-done | bytes 589856 | tf_op jit(solution)/shard_map/ppermute | solution.py:33
  29.8 2.5 %collective-permute-start.13 = (bf16[256,768]{1,0:T(8,128)(2,1)S(1)}, bf16[256,768]{1,0:T(8,128)(2,1)S(1)}, u32[]{:S(2)}, u32[]{:S(2)}) collective-permute-start(bf16[256,768]{1,0:T(8,128)(2,1)S(1)} %get-tuple-element.33), channel_id=1, source_target_pairs={{0,96},{32,0},{64,32},{96,64},{1,97},{33,1},{65,33},{97,65},{2,98}... | collective-permute-start | bytes 1179656 | tf_op jit(solution)/shard_map/ppermute | solution.py:43
  32.3 2.7 %collective-permute-start.6 = (bf16[768,384]{1,0:T(8,128)(2,1)S(1)}, bf16[768,384]{1,0:T(8,128)(2,1)S(1)}, u32[]{:S(2)}, u32[]{:S(2)}) collective-permute-start(bf16[768,384]{1,0:T(8,128)(2,1)S(1)} %pad_maximum_fusion.refs_0_.refs_5_), channel_id=1, source_target_pairs={{0,28},{1,29},{2,30},{3,31},{4,0},{5,1},{6,2},{7,3},{8,4},{9,5},{1... | collective-permute-start | bytes 1769480 | tf_op jit(solution)/shard_map/ppermute | solution.py:33
  35.9 4.4 %collective-permute-done.11.refs_3_ = bf16[256,768]{1,0:T(8,128)(2,1)S(1)} collective-permute-done((bf16[256,768]{1,0:T(8,128)(2,1)S(1)}, bf16[256,768]{1,0:T(8,128)(2,1)S(1)}, u32[]{:S(2)}, u32[]{:S(2)}) %collective-permute-start.11) | collective-permute-done | bytes 393248 | tf_op jit(solution)/shard_map/ppermute | solution.py:43
  40.3 2.0 %collective-permute-start.12 = (bf16[256,768]{1,0:T(8,128)(2,1)S(1)}, bf16[256,768]{1,0:T(8,128)(2,1)S(1)}, u32[]{:S(2)}, u32[]{:S(2)}) collective-permute-start(bf16[256,768]{1,0:T(8,128)(2,1)S(1)} %collective-permute-done.11.refs_3_), channel_id=1, source_target_pairs={{0,128},{128,0},{1,129},{129,1},{2,130},{130,2},{3,131},{131,3},{4... | collective-permute-start | bytes 1179656 | tf_op jit(solution)/shard_map/ppermute | solution.py:47
  42.3 2.9 %collective-permute-start.16 = (bf16[768,384]{1,0:T(8,128)(2,1)S(1)}, bf16[768,384]{1,0:T(8,128)(2,1)S(1)}, u32[]{:S(2)}, u32[]{:S(2)}) collective-permute-start(bf16[768,384]{1,0:T(8,128)(2,1)S(1)} %collective-permute-done.6.refs_2_.refs_7_), channel_id=1, source_target_pairs={{0,28},{1,29},{2,30},{3,31},{4,0},{5,1},{6,2},{7,3},{8,4},{9,5},{1... | collective-permute-start | bytes 1769480 | tf_op jit(solution)/shard_map/ppermute | solution.py:33
  48.5 3.6 %collective-permute-done.16.refs_4_.refs_9_ = bf16[768,384]{1,0:T(8,128)(2,1)S(1)} collective-permute-done((bf16[768,384]{1,0:T(8,128)(2,1)S(1)}, bf16[768,384]{1,0:T(8,128)(2,1)S(1)}, u32[]{:S(2)}, u32[]{:S(2)}) %collective-permute-start.16) | collective-permute-done | bytes 589856 | tf_op jit(solution)/shard_map/ppermute | solution.py:33
  52.1 3.4 %collective-permute-done.15.refs_5_.refs_10_ = bf16[768,384]{1,0:T(8,128)(2,1)S(1)} collective-permute-done((bf16[768,384]{1,0:T(8,128)(2,1)S(1)}, bf16[768,384]{1,0:T(8,128)(2,1)S(1)}, u32[]{:S(2)}, u32[]{:S(2)}) %collective-permute-start.15) | collective-permute-done | bytes 589856 | tf_op jit(solution)/shard_map/ppermute | solution.py:33
  56.9 7.6 %collective-permute-done.17.refs_6_.refs_11_ = bf16[768,384]{1,0:T(8,128)(2,1)S(1)} collective-permute-done((bf16[768,384]{1,0:T(8,128)(2,1)S(1)}, bf16[768,384]{1,0:T(8,128)(2,1)S(1)}, u32[]{:S(2)}, u32[]{:S(2)}) %collective-permute-start.17) | collective-permute-done | bytes 589856 | tf_op jit(solution)/shard_map/ppermute | solution.py:33
  65.9 3.6 %collective-permute-start.20 = (bf16[1536,384]{1,0:T(8,128)(2,1)S(1)}, bf16[1536,384]{1,0:T(8,128)(2,1)S(1)}, u32[]{:S(2)}, u32[]{:S(2)}) collective-permute-start(bf16[1536,384]{1,0:T(8,128)(2,1)S(1)} %query_half.1.w_own), channel_id=1, source_target_pairs={{0,128},{128,0},{1,129},{129,1},{2,130},{130,2},{3,131},{131,3},{4... | collective-permute-start | bytes 3538952 | tf_op jit(solution)/shard_map/ppermute | solution.py:47
  69.5 2.2 %project_cross.1 = (bf16[512,384]{1,0:T(8,128)(2,1)S(1)}, bf16[3072,384]{1,0:T(8,128)(2,1)S(1)}) custom-call(f32[2,128]{1,0:T(2,128)S(1)} %copy-done, bf16[512,768]{1,0:T(8,128)(2,1)S(1)} %collective-permute-done.8.refs_0_, bf16[512,768]{1,0:T(8,128)(2,1)S(1)} %collective-permute-done.9.refs_1_, bf16[512,768]{1,0:T(8,128)(2,1)S(1)} %collective-permute-done.10.refs_2_, ...), custom_call_target="tpu_custom_call" | custom-call | flops 1207959552 | bytes 6291456 | tf_op jit(solution)/shard_map/project_cross/pallas_call | solution.py:114
  76.1 3.0 %query.1 = (bf16[512,384]{1,0:T(8,128)(2,1)S(1)}, f32[3,512,256]{2,1,0:T(8,128)S(1)}) custom-call(f32[2,128]{1,0:T(2,128)S(1)} %copy-done, s32[4,10]{1,0:T(4,128)S(1)} %copy-done.4, bf16[1536,384]{1,0:T(8,128)(2,1)S(1)} %query_half.1.w_own, bf16[1536,384]{1,0:T(8,128)(2,1)S(1)} %collective-permute-done.20.w_other, bf16[512,768]{1,0:T(8,128)(2,1)S(1)} %copy-done.1, ...), custom_call_target="tpu_custom_call" | custom-call | flops 34359738368 | bytes 6291456 | tf_op jit(solution)/shard_map/query/pallas_call | solution.py:114
  79.2 8.9 %collective-permute-done.23.after = bf16[512,512]{1,0:T(8,128)(2,1)S(1)} collective-permute-done((bf16[512,512]{1,0:T(8,128)(2,1)S(1)}, bf16[512,512]{1,0:T(8,128)(2,1)S(1)}, u32[]{:S(2)}, u32[]{:S(2)}) %collective-permute-start.23) | collective-permute-done | bytes 524320 | tf_op jit(solution)/shard_map/ppermute | solution.py:38
  88.0 3.4 %collective-permute-done.22.before = bf16[512,512]{1,0:T(8,128)(2,1)S(1)} collective-permute-done((bf16[512,512]{1,0:T(8,128)(2,1)S(1)}, bf16[512,512]{1,0:T(8,128)(2,1)S(1)}, u32[]{:S(2)}, u32[]{:S(2)}) %collective-permute-start.22) | collective-permute-done | bytes 524320 | tf_op jit(solution)/shard_map/ppermute | solution.py:38
  92.8 2.0 %collective-permute-start.25 = (bf16[512,256]{1,0:T(8,128)(2,1)S(1)}, bf16[512,256]{1,0:T(8,128)(2,1)S(1)}, u32[]{:S(2)}, u32[]{:S(2)}) collective-permute-start(bf16[512,256]{1,0:T(8,128)(2,1)S(1)} %attend_0.1.refs_0_), channel_id=1, source_target_pairs={{0,96},{32,0},{64,32},{96,64},{1,97},{33,1},{65,33},{97,65},{2,98}... | collective-permute-start | bytes 786440 | tf_op jit(solution)/shard_map/ppermute | solution.py:43
  96.2 3.2 %collective-permute-done.25.refs_2_ = bf16[512,256]{1,0:T(8,128)(2,1)S(1)} collective-permute-done((bf16[512,256]{1,0:T(8,128)(2,1)S(1)}, bf16[512,256]{1,0:T(8,128)(2,1)S(1)}, u32[]{:S(2)}, u32[]{:S(2)}) %collective-permute-start.25) | collective-permute-done | bytes 262176 | tf_op jit(solution)/shard_map/ppermute | solution.py:43
  99.4 3.1 %collective-permute-start.27 = (bf16[256,256]{1,0:T(8,128)(2,1)S(1)}, bf16[256,256]{1,0:T(8,128)(2,1)S(1)}, u32[]{:S(2)}, u32[]{:S(2)}) collective-permute-start(bf16[256,256]{1,0:T(8,128)(2,1)S(1)} %slice.9), channel_id=1, source_target_pairs={{0,96},{32,0},{64,32},{96,64},{1,97},{33,1},{65,33},{97,65},{2,98}... | collective-permute-start | bytes 393224 | tf_op jit(solution)/shard_map/ppermute | solution.py:43
  102.7 2.0 %collective-permute-done.28.before = bf16[512,256]{1,0:T(8,128)(2,1)S(1)} collective-permute-done((bf16[512,256]{1,0:T(8,128)(2,1)S(1)}, bf16[512,256]{1,0:T(8,128)(2,1)S(1)}, u32[]{:S(2)}, u32[]{:S(2)}) %collective-permute-start.28) | collective-permute-done | bytes 262176 | tf_op jit(solution)/shard_map/ppermute | solution.py:38
  112.6 2.3 %collective-permute-done.30.refs_1_ = bf16[512,128]{1,0:T(8,128)(2,1)S(1)} collective-permute-done((bf16[512,128]{1,0:T(8,128)(2,1)S(1)}, bf16[512,128]{1,0:T(8,128)(2,1)S(1)}, u32[]{:S(2)}, u32[]{:S(2)}) %collective-permute-start.30) | collective-permute-done | bytes 131104 | tf_op jit(solution)/shard_map/ppermute | solution.py:43
  (67 shorter events, 26.7 us)
Async XLA Ops:
  0.0 22.8 %collective-permute-start.1 = (bf16[512,768]{1,0:T(8,128)(2,1)}, bf16[512,768]{1,0:T(8,128)(2,1)S(1)}, u32[]{:S(2)}, u32[]{:S(2)}) collective-permute-start(bf16[512,768]{1,0:T(8,128)(2,1)} %refs_0_.3), channel_id=1, source_target_pairs={{0,96},{32,0},{64,32},{96,64},{1,97},{33,1},{65,33},{97,65},{2,98}... | collective-permute-start | bytes 2359304 | tf_op jit(solution)/shard_map/ppermute | solution.py:43
  3.3 19.5 %collective-permute-start = (bf16[512,768]{1,0:T(8,128)(2,1)}, bf16[512,768]{1,0:T(8,128)(2,1)S(1)}, u32[]{:S(2)}, u32[]{:S(2)}) collective-permute-start(bf16[512,768]{1,0:T(8,128)(2,1)} %refs_0_.3), channel_id=1, source_target_pairs={{0,32},{32,64},{64,96},{96,0},{1,33},{33,65},{65,97},{97,1},{2,34}... | collective-permute-start | bytes 2359304 | tf_op jit(solution)/shard_map/ppermute | solution.py:43
  5.2 9.6 %collective-permute-start.4 = (bf16[192,384]{1,0:T(8,128)(2,1)S(1)}, bf16[192,384]{1,0:T(8,128)(2,1)S(1)}, u32[]{:S(2)}, u32[]{:S(2)}) collective-permute-start(bf16[192,384]{1,0:T(8,128)(2,1)S(1)} %prepare.1), channel_id=1, source_target_pairs={{0,2},{1,3},{2,0},{3,1},{4,6},{5,7},{6,4},{7,5},{8,10},{9,11},{10,... | collective-permute-start | bytes 442376 | tf_op jit(solution)/shard_map/ppermute | solution.py:33
  12.2 8.0 %collective-permute-start.3 = (bf16[192,384]{1,0:T(8,128)(2,1)S(1)}, bf16[192,384]{1,0:T(8,128)(2,1)S(1)}, u32[]{:S(2)}, u32[]{:S(2)}) collective-permute-start(bf16[192,384]{1,0:T(8,128)(2,1)S(1)} %prepare.1), channel_id=1, source_target_pairs={{0,3},{1,0},{2,1},{3,2},{4,7},{5,4},{6,5},{7,6},{8,11},{9,8},{10,9... | collective-permute-start | bytes 442376 | tf_op jit(solution)/shard_map/ppermute | solution.py:33
  12.2 8.0 %collective-permute-start.2 = (bf16[192,384]{1,0:T(8,128)(2,1)S(1)}, bf16[192,384]{1,0:T(8,128)(2,1)S(1)}, u32[]{:S(2)}, u32[]{:S(2)}) collective-permute-start(bf16[192,384]{1,0:T(8,128)(2,1)S(1)} %prepare.1), channel_id=1, source_target_pairs={{0,1},{1,2},{2,3},{3,0},{4,5},{5,6},{6,7},{7,4},{8,9},{9,10},{10,1... | collective-permute-start | bytes 442376 | tf_op jit(solution)/shard_map/ppermute | solution.py:33
  14.8 20.2 %collective-permute-start.8 = (bf16[512,768]{1,0:T(8,128)(2,1)S(1)}, bf16[512,768]{1,0:T(8,128)(2,1)S(1)}, u32[]{:S(2)}, u32[]{:S(2)}) collective-permute-start(bf16[512,768]{1,0:T(8,128)(2,1)S(1)} %copy-done.1), channel_id=1, source_target_pairs={{0,128},{128,0},{1,129},{129,1},{2,130},{130,2},{3,131},{131,3},{4... | collective-permute-start | bytes 2359304 | tf_op jit(solution)/shard_map/ppermute | solution.py:47
  20.3 9.3 %collective-permute-start.5 = (bf16[768,384]{1,0:T(8,128)(2,1)S(1)}, bf16[768,384]{1,0:T(8,128)(2,1)S(1)}, u32[]{:S(2)}, u32[]{:S(2)}) collective-permute-start(bf16[768,384]{1,0:T(8,128)(2,1)S(1)} %pad_maximum_fusion.refs_0_.refs_5_), channel_id=1, source_target_pairs={{0,4},{1,5},{2,6},{3,7},{4,8},{5,9},{6,10},{7,11},{8,12},{9,13},{1... | collective-permute-start | bytes 1769480 | tf_op jit(solution)/shard_map/ppermute | solution.py:33
  29.6 10.7 %collective-permute-start.11 = (bf16[256,768]{1,0:T(8,128)(2,1)S(1)}, bf16[256,768]{1,0:T(8,128)(2,1)S(1)}, u32[]{:S(2)}, u32[]{:S(2)}) collective-permute-start(bf16[256,768]{1,0:T(8,128)(2,1)S(1)} %get-tuple-element.32), channel_id=1, source_target_pairs={{0,32},{32,64},{64,96},{96,0},{1,33},{33,65},{65,97},{97,1},{2,34}... | collective-permute-start | bytes 1179656 | tf_op jit(solution)/shard_map/ppermute | solution.py:43
  29.8 12.5 %collective-permute-start.13 = (bf16[256,768]{1,0:T(8,128)(2,1)S(1)}, bf16[256,768]{1,0:T(8,128)(2,1)S(1)}, u32[]{:S(2)}, u32[]{:S(2)}) collective-permute-start(bf16[256,768]{1,0:T(8,128)(2,1)S(1)} %get-tuple-element.33), channel_id=1, source_target_pairs={{0,96},{32,0},{64,32},{96,64},{1,97},{33,1},{65,33},{97,65},{2,98}... | collective-permute-start | bytes 1179656 | tf_op jit(solution)/shard_map/ppermute | solution.py:43
  32.3 10.1 %collective-permute-start.6 = (bf16[768,384]{1,0:T(8,128)(2,1)S(1)}, bf16[768,384]{1,0:T(8,128)(2,1)S(1)}, u32[]{:S(2)}, u32[]{:S(2)}) collective-permute-start(bf16[768,384]{1,0:T(8,128)(2,1)S(1)} %pad_maximum_fusion.refs_0_.refs_5_), channel_id=1, source_target_pairs={{0,28},{1,29},{2,30},{3,31},{4,0},{5,1},{6,2},{7,3},{8,4},{9,5},{1... | collective-permute-start | bytes 1769480 | tf_op jit(solution)/shard_map/ppermute | solution.py:33
  35.0 10.2 %collective-permute-start.7 = (bf16[768,384]{1,0:T(8,128)(2,1)S(1)}, bf16[768,384]{1,0:T(8,128)(2,1)S(1)}, u32[]{:S(2)}, u32[]{:S(2)}) collective-permute-start(bf16[768,384]{1,0:T(8,128)(2,1)S(1)} %collective-permute-done.5.refs_1_.refs_6_), channel_id=1, source_target_pairs={{0,4},{1,5},{2,6},{3,7},{4,8},{5,9},{6,10},{7,11},{8,12},{9,13},{1... | collective-permute-start | bytes 1769480 | tf_op jit(solution)/shard_map/ppermute | solution.py:33
  35.0 13.5 %collective-permute-start.9 = (bf16[512,768]{1,0:T(8,128)(2,1)S(1)}, bf16[512,768]{1,0:T(8,128)(2,1)S(1)}, u32[]{:S(2)}, u32[]{:S(2)}) collective-permute-start(bf16[512,768]{1,0:T(8,128)(2,1)S(1)} %collective-permute-done.below.refs_1_), channel_id=1, source_target_pairs={{0,128},{128,0},{1,129},{129,1},{2,130},{130,2},{3,131},{131,3},{4... | collective-permute-start | bytes 2359304 | tf_op jit(solution)/shard_map/ppermute | solution.py:47
  42.3 9.7 %collective-permute-start.16 = (bf16[768,384]{1,0:T(8,128)(2,1)S(1)}, bf16[768,384]{1,0:T(8,128)(2,1)S(1)}, u32[]{:S(2)}, u32[]{:S(2)}) collective-permute-start(bf16[768,384]{1,0:T(8,128)(2,1)S(1)} %collective-permute-done.6.refs_2_.refs_7_), channel_id=1, source_target_pairs={{0,28},{1,29},{2,30},{3,31},{4,0},{5,1},{6,2},{7,3},{8,4},{9,5},{1... | collective-permute-start | bytes 1769480 | tf_op jit(solution)/shard_map/ppermute | solution.py:33
  45.2 10.2 %collective-permute-start.15 = (bf16[768,384]{1,0:T(8,128)(2,1)S(1)}, bf16[768,384]{1,0:T(8,128)(2,1)S(1)}, u32[]{:S(2)}, u32[]{:S(2)}) collective-permute-start(bf16[768,384]{1,0:T(8,128)(2,1)S(1)} %collective-permute-done.7.refs_3_.refs_8_), channel_id=1, source_target_pairs={{0,4},{1,5},{2,6},{3,7},{4,8},{5,9},{6,10},{7,11},{8,12},{9,13},{1... | collective-permute-start | bytes 1769480 | tf_op jit(solution)/shard_map/ppermute | solution.py:33
  55.5 9.0 %collective-permute-start.17 = (bf16[768,384]{1,0:T(8,128)(2,1)S(1)}, bf16[768,384]{1,0:T(8,128)(2,1)S(1)}, u32[]{:S(2)}, u32[]{:S(2)}) collective-permute-start(bf16[768,384]{1,0:T(8,128)(2,1)S(1)} %collective-permute-done.16.refs_4_.refs_9_), channel_id=1, source_target_pairs={{0,28},{1,29},{2,30},{3,31},{4,0},{5,1},{6,2},{7,3},{8,4},{9,5},{1... | collective-permute-start | bytes 1769480 | tf_op jit(solution)/shard_map/ppermute | solution.py:33
  55.5 10.2 %collective-permute-start.18 = (bf16[768,384]{1,0:T(8,128)(2,1)S(1)}, bf16[768,384]{1,0:T(8,128)(2,1)S(1)}, u32[]{:S(2)}, u32[]{:S(2)}) collective-permute-start(bf16[768,384]{1,0:T(8,128)(2,1)S(1)} %collective-permute-done.15.refs_5_.refs_10_), channel_id=1, source_target_pairs={{0,4},{1,5},{2,6},{3,7},{4,8},{5,9},{6,10},{7,11},{8,12},{9,13},{1... | collective-permute-start | bytes 1769480 | tf_op jit(solution)/shard_map/ppermute | solution.py:33
  65.9 10.2 %collective-permute-start.20 = (bf16[1536,384]{1,0:T(8,128)(2,1)S(1)}, bf16[1536,384]{1,0:T(8,128)(2,1)S(1)}, u32[]{:S(2)}, u32[]{:S(2)}) collective-permute-start(bf16[1536,384]{1,0:T(8,128)(2,1)S(1)} %query_half.1.w_own), channel_id=1, source_target_pairs={{0,128},{128,0},{1,129},{129,1},{2,130},{130,2},{3,131},{131,3},{4... | collective-permute-start | bytes 3538952 | tf_op jit(solution)/shard_map/ppermute | solution.py:47
  72.0 36.0 %collective-permute-start.19 = (bf16[1536,384]{1,0:T(8,128)(2,1)S(1)}, bf16[1536,384]{1,0:T(8,128)(2,1)S(1)}, u32[]{:S(2)}, u32[]{:S(2)}) collective-permute-start(bf16[1536,384]{1,0:T(8,128)(2,1)S(1)} %out_half.1.w_own), channel_id=1, source_target_pairs={{0,128},{128,0},{1,129},{129,1},{2,130},{130,2},{3,131},{131,3},{4... | collective-permute-start | bytes 3538952 | tf_op jit(solution)/shard_map/ppermute | solution.py:47
  74.6 13.5 %collective-permute-start.23 = (bf16[512,512]{1,0:T(8,128)(2,1)S(1)}, bf16[512,512]{1,0:T(8,128)(2,1)S(1)}, u32[]{:S(2)}, u32[]{:S(2)}) collective-permute-start(bf16[512,512]{1,0:T(8,128)(2,1)S(1)} %get-tuple-element.43.refs_5_), channel_id=1, source_target_pairs={{0,31},{1,0},{2,1},{3,2},{4,3},{5,4},{6,5},{7,6},{8,7},{9,8},{10,9... | collective-permute-start | bytes 1572872 | tf_op jit(solution)/shard_map/ppermute | solution.py:38
  74.9 16.5 %collective-permute-start.22 = (bf16[512,512]{1,0:T(8,128)(2,1)S(1)}, bf16[512,512]{1,0:T(8,128)(2,1)S(1)}, u32[]{:S(2)}, u32[]{:S(2)}) collective-permute-start(bf16[512,512]{1,0:T(8,128)(2,1)S(1)} %get-tuple-element.43.refs_5_), channel_id=1, source_target_pairs={{0,1},{1,2},{2,3},{3,4},{4,5},{5,6},{6,7},{7,8},{8,9},{9,10},{10,1... | collective-permute-start | bytes 1572872 | tf_op jit(solution)/shard_map/ppermute | solution.py:38
  94.7 7.8 %collective-permute-start.24 = (bf16[512,256]{1,0:T(8,128)(2,1)S(1)}, bf16[512,256]{1,0:T(8,128)(2,1)S(1)}, u32[]{:S(2)}, u32[]{:S(2)}) collective-permute-start(bf16[512,256]{1,0:T(8,128)(2,1)S(1)} %attend_0.1.refs_0_), channel_id=1, source_target_pairs={{0,32},{32,64},{64,96},{96,0},{1,33},{33,65},{65,97},{97,1},{2,34}... | collective-permute-start | bytes 786440 | tf_op jit(solution)/shard_map/ppermute | solution.py:43
  94.7 7.9 %collective-permute-start.29 = (bf16[512,256]{1,0:T(8,128)(2,1)S(1)}, bf16[512,256]{1,0:T(8,128)(2,1)S(1)}, u32[]{:S(2)}, u32[]{:S(2)}) collective-permute-start(bf16[512,256]{1,0:T(8,128)(2,1)S(1)} %get-tuple-element.44.refs_6_), channel_id=1, source_target_pairs={{0,31},{1,0},{2,1},{3,2},{4,3},{5,4},{6,5},{7,6},{8,7},{9,8},{10,9... | collective-permute-start | bytes 786440 | tf_op jit(solution)/shard_map/ppermute | solution.py:38
  95.1 9.6 %collective-permute-start.28 = (bf16[512,256]{1,0:T(8,128)(2,1)S(1)}, bf16[512,256]{1,0:T(8,128)(2,1)S(1)}, u32[]{:S(2)}, u32[]{:S(2)}) collective-permute-start(bf16[512,256]{1,0:T(8,128)(2,1)S(1)} %get-tuple-element.44.refs_6_), channel_id=1, source_target_pairs={{0,1},{1,2},{2,3},{3,4},{4,5},{5,6},{6,7},{7,8},{8,9},{9,10},{10,1... | collective-permute-start | bytes 786440 | tf_op jit(solution)/shard_map/ppermute | solution.py:38
  99.4 9.1 %collective-permute-start.27 = (bf16[256,256]{1,0:T(8,128)(2,1)S(1)}, bf16[256,256]{1,0:T(8,128)(2,1)S(1)}, u32[]{:S(2)}, u32[]{:S(2)}) collective-permute-start(bf16[256,256]{1,0:T(8,128)(2,1)S(1)} %slice.9), channel_id=1, source_target_pairs={{0,96},{32,0},{64,32},{96,64},{1,97},{33,1},{65,33},{97,65},{2,98}... | collective-permute-start | bytes 393224 | tf_op jit(solution)/shard_map/ppermute | solution.py:43
  (14 other events, 102.8 us)
where the time goes:
time: 117 us
  waiting for transfers between devices  56.4 us (48%)
  starting transfers between devices  45.2 us (39%)
  Pallas kernels  13.1 us (11%)
  local copies, waits for them, and re-layouts  1.85 us (2%)
    ppermute x10, waiting for transfers between devices, moved(): return lax.ppermute(x, ('dp', 'head'), pairs)  28.1 us
    ppermute x10, starting transfers between devices, moved(): return lax.ppermute(x, ('dp', 'head'), pairs)  19 us
    ppermute x11, starting transfers between devices, along(): return lax.ppermute(x, axis, [(i, (i + step) % n) for i in range(n)])  14.2 us
    ppermute x4, waiting for transfers between devices, frames_on(): return lax.ppermute(x, 'head', [(i, (i + step) % n) for i in range(n)])  14.2 us
    pallas_call x12, Pallas kernels, call(): pl.pallas_call(kernel, out_shape=out_shape, in_specs=[VMEM] * n, out_spec...  13.1 us
    ppermute x11, waiting for transfers between devices, along(): return lax.ppermute(x, axis, [(i, (i + step) % n) for i in range(n)])  12.6 us
    ppermute x8, starting transfers between devices, swapped(): return lax.ppermute(x, 'dp', [(0, 1), (1, 0)])  9 us
    ppermute x4, starting transfers between devices, frames_on(): return lax.ppermute(x, 'head', [(i, (i + step) % n) for i in range(n)])  3.01 us
  transfers between devices with their start and end apart: 33, of which 17 were waited for; matrix products, arithmetic and copies ran while one was open for 0% of the time, Pallas kernels for 10%

commit v1 on v0

--- a/solution.py
+++ b/solution.py
@@ -33,9 +33,13 @@
     return lax.ppermute(x, ("dp", "head"), pairs)
 
 
-def frames_on(x, step):
+def frames_on(x, step, cross):
     n = NZ * NY
-    return lax.ppermute(x, "head", [(i, (i + step) % n) for i in range(n)])
+    pairs = []
+    for core in range(2):
+        to = 1 - core if cross else core
+        pairs += [(core * n + i, to * n + (i + step) % n) for i in range(n)]
+    return lax.ppermute(x, ("dp", "head"), pairs)
 
 
 def along(x, axis, step):
@@ -145,55 +149,59 @@
     store(slice(half, 2 * half), near[half:] + part(far_bottom, 2))
 
 
-def kv_store(out, core, gains):
+def kv_store(outs, core, gains):
     def store(rows, product):
-        for h in range(product.shape[1] // HD):
-            at = slice(h * HD, (h + 1) * HD)
-            part = product[:, at]
-            out[rows, at] = jnp.where(core == 0, normed(part, gains[1:2, :]), part.astype(BF))
+        for out, group in zip(outs, GROUPS, strict=True):
+            for n, h in enumerate(group):
+                part = product[:, h * HD : (h + 1) * HD]
+                out[rows, n * HD : (n + 1) * HD] = jnp.where(
+                    core == 0, normed(part, gains[1:2, :]), part.astype(BF)
+                )
 
     return store
 
 
 def cross_kernel(gains, *refs):
     pieces, buffers = refs[:5], refs[5:13]
-    out, w = refs[13:]
+    outs, w = refs[13:-1], refs[-1]
     core, seq, z, y = place()
-    rows = w.shape[0] // (NZ * NY)
-    assemble(w, buffers, 0, rows, core, z, y)
-    multiply_tokens(pieces, w, seq, kv_store(out, core, gains))
+    assemble(w, buffers, 0, w.shape[0] // (NZ * NY), core, z, y)
+    multiply_tokens(pieces, w, seq, kv_store(outs, core, gains))
 
 
 def same_kernel(gains, *refs):
-    pieces, w, out = refs[:5], refs[5], refs[6]
+    pieces, w, outs = refs[:5], refs[5], refs[6:]
     core, seq, _, _ = place()
-    multiply_tokens(pieces, w, seq, kv_store(out, core, gains))
-
-
-def pack_kernel(a, b, *outs):
+    multiply_tokens(pieces, w, seq, kv_store(outs, core, gains))
+
+
+def pack_kernel(a, b, out):
     core = lax.axis_index("dp")
-    for out, group in zip(outs, GROUPS, strict=True):
-        at = slice(group[0] * HD, (group[-1] + 1) * HD)
-        size = len(group) * HD
-        out[:, :size] = jnp.where(core == 0, a[:, at], b[:, at])
-        out[:, size:] = jnp.where(core == 0, b[:, at], a[:, at])
-
-
-def project_kv(gains, tokens, others, buffers):
+    size = a.shape[1]
+    out[:, :size] = jnp.where(core == 0, a[...], b[...])
+    out[:, size:] = jnp.where(core == 0, b[...], a[...])
+
+
+def group_shapes(rows):
+    return tuple(jax.ShapeDtypeStruct((rows, len(g) * HD), BF) for g in GROUPS)
+
+
+def project_cross(gains, others, buffers):
+    rows, feats = others[0].shape
+    depth, width = NX * feats, buffers[0].shape[1]
+    return call(
+        cross_kernel,
+        (*group_shapes(rows), jax.ShapeDtypeStruct((depth, width), BF)),
+        (gains, *others, *buffers), [], 2 * rows * depth * width, 6 * 2**20, 20, "project_cross",
+    )
+
+
+def project_same(gains, tokens, w):
     rows, feats = tokens[0].shape
-    depth, width = NX * feats, buffers[0].shape[1]
-    part = jax.ShapeDtypeStruct((rows, width), BF)
-    flops = 2 * rows * depth * width
-    cross, w = call(
-        cross_kernel, (part, jax.ShapeDtypeStruct((depth, width), BF)),
-        (gains, *others, *buffers), [], flops, 6 * 2**20, 20, "project_cross",
-    )
-    cross = swapped(cross)
-    same = call(same_kernel, part, (gains, *tokens, w), [], 8 * flops, 6 * 2**20, 20, "project_same")
+    depth, width = w.shape
     return call(
-        pack_kernel,
-        tuple(jax.ShapeDtypeStruct((rows, 2 * len(g) * HD), BF) for g in GROUPS),
-        (same, cross), [], 0, 2**21, 8, "pack",
+        same_kernel, group_shapes(rows), (gains, *tokens, w),
+        [], 2 * rows * depth * width, 6 * 2**20, 20, "project_same",
     )
 
 
@@ -211,16 +219,24 @@
     )
 
 
-def attend_frame(scale, q, kv, keep, n):
-    rows, keys = q.shape[0], kv.shape[0]
-    at, size = n * HD, kv.shape[1] // 2
-    score = lax.dot_general(
-        q, kv[:, at : at + HD], (((1,), (1,)), ((), ())), preferred_element_type=F32
-    )
+def attend_frame(scale, q, key, value, keep):
+    rows, keys = q.shape[0], key.shape[0]
+    score = lax.dot_general(q, key, (((1,), (1,)), ((), ())), preferred_element_type=F32)
     weight = jnp.exp2(score * scale).reshape(rows // TILE, TILE, keys)
     weight = jnp.where(keep[:, None, :] > 0, weight, 0.0).reshape(rows, keys).astype(BF)
-    value = jnp.concatenate([kv[:, size + at : size + at + HD], jnp.ones((keys, HD), BF)], axis=1)
+    value = jnp.concatenate([value, jnp.ones((keys, HD), BF)], axis=1)
     return jnp.dot(weight, value, preferred_element_type=F32)
+
+
+def picked(a, b, n):
+    core = lax.axis_index("dp")
+    at = slice(n * HD, (n + 1) * HD)
+    return jnp.where(core == 0, a[:, at], b[:, at]), jnp.where(core == 0, b[:, at], a[:, at])
+
+
+def unpacked(kv, n):
+    size = kv.shape[1] // 2
+    return kv[:, n * HD : (n + 1) * HD], kv[:, size + n * HD : size + (n + 1) * HD]
 
 
 def kept(listed, frame, keys):
@@ -233,9 +249,8 @@
     return jnp.where(keep & (tile >= 0), 1.0, 0.0)
 
 
-def q_kernel(scale, gains, near, w_own, w_other, *refs):
-    pieces, kvs = refs[:5], refs[5 : 5 + len(GROUPS)]
-    q_ref, acc, w = refs[5 + len(GROUPS) :]
+def q_kernel(gains, w_own, w_other, *refs):
+    pieces, q_ref, w = refs[:5], refs[5], refs[6]
     core, seq, _, _ = place()
     rows = w.shape[0] // (2 * NZ * NY)
     for block in range(NZ * NY):
@@ -251,19 +266,30 @@
             q_ref[span, at] = normed(product[:, at], gains[0:1, :])
 
     multiply_tokens(pieces, w, seq, store)
+
+
+def own_kernel(scale, near, q_ref, *refs):
+    acc = refs[-1]
     keep = kept(near[...], lax.axis_index("head"), q_ref.shape[0])
-    for kv, group in zip(kvs, GROUPS, strict=True):
+    for g, group in enumerate(GROUPS):
         for n, h in enumerate(group):
-            acc[h] = attend_frame(scale, q_ref[:, h * HD : (h + 1) * HD], kv, keep, n)
-
-
-def attend_kernel(scale, group, near, q_ref, acc, before, after, out):
+            key, value = picked(refs[2 * g], refs[2 * g + 1], n)
+            acc[h] = attend_frame(scale, q_ref[:, h * HD : (h + 1) * HD], key, value, keep)
+
+
+def attend_kernel(scale, group, near, q_ref, acc, *refs):
+    sides, out = refs[:-1], refs[-1]
     head = lax.axis_index("head")
     keep = [kept(near[...], head + step, q_ref.shape[0]) for step in (-1, 1)]
     for n, h in enumerate(group):
         q = q_ref[:, h * HD : (h + 1) * HD]
-        total = acc[h] + attend_frame(scale, q, before, keep[0], n)
-        total = total + attend_frame(scale, q, after, keep[1], n)
+        total = acc[h]
+        for j in range(2):
+            if len(sides) == 4:
+                key, value = picked(sides[2 * j], sides[2 * j + 1], n)
+            else:
+                key, value = unpacked(sides[j], n)
+            total = total + attend_frame(scale, q, key, value, keep[j])
         out[:, n * HD : (n + 1) * HD] = (total[:, :HD] / total[:, HD:]).astype(BF)
 
 
@@ -317,19 +343,31 @@
     )
     tokens, others, buffers = gathered(tokens_in, mine)
 
-    kv = project_kv(norm_gains, tokens, others, buffers)
-    sides = [[frames_on(x, step) for step in (1, -1)] for x in kv]
+    w_q = half_of(buffers, depth, depth // 2, "query_half")
+    w_q_other = swapped(w_q)
+    *cross, w = project_cross(norm_gains, others, buffers)
+    others_kv = [swapped(x) for x in cross]
+    b0, b1 = (frames_on(cross[0], step, True) for step in (1, -1))
+    gains, w, *others_kv = lax.optimization_barrier((norm_gains, w, *others_kv))
+    same = project_same(gains, tokens, w)
+    a0, a1 = (frames_on(same[0], step, False) for step in (1, -1))
+    query = call(
+        q_kernel, jax.ShapeDtypeStruct((rows, width), BF),
+        (norm_gains, w_q, w_q_other, *tokens),
+        [pltpu.VMEM((NX * feats, width), BF)], 2**35, 6 * 2**20, 20, "query",
+    )
+    late, _ = lax.optimization_barrier((same[1], query))
+    packed = call(
+        pack_kernel, jax.ShapeDtypeStruct((rows, 2 * late.shape[1]), BF),
+        (late, others_kv[1]), [], 0, 2**19, 8, "pack",
+    )
+    sides = [(a0, b0, a1, b1), tuple(frames_on(packed, step, False) for step in (1, -1))]
     scale = HD ** (-0.5) * math.log2(math.e)
-    w_q = half_of(buffers, depth, depth // 2, "query_half")
-    query, acc = call(
-        functools.partial(q_kernel, scale),
-        (
-            jax.ShapeDtypeStruct((rows, width), BF),
-            jax.ShapeDtypeStruct((heads, rows, 2 * HD), F32),
-        ),
-        (norm_gains, neighbours, w_q, swapped(w_q), *tokens, *kv),
-        [pltpu.VMEM((NX * feats, width), BF)],
-        2**35, 6 * 2**20, 20, "query",
+    acc = call(
+        functools.partial(own_kernel, scale),
+        jax.ShapeDtypeStruct((heads, rows, 2 * HD), F32),
+        (neighbours, query, same[0], others_kv[0], same[1], others_kv[1]),
+        [], 2**35, 6 * 2**20, 20, "own_frame",
     )
     first = depth * 3 // 2
     w_out = half_of(buffers, first, mine.shape[0] - first, "out_half")
@@ -341,9 +379,9 @@
             functools.partial(attend_kernel, scale, group),
             jax.ShapeDtypeStruct((rows, len(group) * HD), BF),
             (neighbours, query, acc, *sides[g]),
-            [], (2**35 if not last else 2**30), 4 * 2**20, 16, "attend_%d" % g,
+            [], 2**30, 4 * 2**20, 16, "attend_%d" % g,
         )
-        pieces = (direct_x if last and g else ring_x)(out)
+        pieces = direct_x(out)
         total = (
             call(
                 functools.partial(output_kernel if g else first_kernel, group),

time: 117 us -> 114 us (0.974)
  waiting for transfers between devices: 56.4 us -> 47.7 us
  starting transfers between devices: 45.2 us -> 51.4 us
    ppermute x4 -> x6, waiting for transfers between devices: 14.2 us -> 3.84 us  [frames_on(): return lax.ppermute(x, ('dp', 'head'), pairs)]
    ppermute x4 -> x6, starting transfers between devices: 3.01 us -> 10.3 us  [frames_on(): return lax.ppermute(x, ('dp', 'head'), pairs)]
    ppermute x11 -> x10, waiting for transfers between devices: 12.6 us -> 14.4 us  [along(): return lax.ppermute(x, axis, [(i, (i + step) % n) for i in range(n)])]
    ppermute x11 -> x10, starting transfers between devices: 14.2 us -> 12.9 us  [along(): return lax.ppermute(x, axis, [(i, (i + step) % n) for i in range(n)])]
    ppermute x8 -> x9, starting transfers between devices: 9 us -> 9.19 us  [swapped(): return lax.ppermute(x, 'dp', [(0, 1), (1, 0)])]
    pallas_call x12 -> x13, Pallas kernels: 13.1 us -> 13.1 us  [call(): pl.pallas_call(kernel, out_shape=out_shape, in_specs=[VMEM] * n, out_spec...]
  transfers between devices with their start and end apart: 33 -> 35, of which waited for: 17 -> 16; matrix products, arithmetic and copies ran while one was open for 0% -> 0% of each run, Pallas kernels for 10% -> 10%
where the time goes in v1:
time: 114 us
  starting transfers between devices  51.4 us (45%)
  waiting for transfers between devices  47.7 us (42%)
  Pallas kernels  13.1 us (11%)
  local copies, waits for them, and re-layouts  1.83 us (2%)
    ppermute x10, waiting for transfers between devices, moved(): return lax.ppermute(x, ('dp', 'head'), pairs)  28.1 us
    ppermute x10, starting transfers between devices, moved(): return lax.ppermute(x, ('dp', 'head'), pairs)  19 us
    ppermute x10, waiting for transfers between devices, along(): return lax.ppermute(x, axis, [(i, (i + step) % n) for i in range(n)])  14.4 us
    pallas_call x13, Pallas kernels, call(): pl.pallas_call(kernel, out_shape=out_shape, in_specs=[VMEM] * n, out_spec...  13.1 us
    ppermute x10, starting transfers between devices, along(): return lax.ppermute(x, axis, [(i, (i + step) % n) for i in range(n)])  12.9 us
    ppermute x6, starting transfers between devices, frames_on(): return lax.ppermute(x, ('dp', 'head'), pairs)  10.3 us
    ppermute x9, starting transfers between devices, swapped(): return lax.ppermute(x, 'dp', [(0, 1), (1, 0)])  9.19 us
    ppermute x6, waiting for transfers between devices, frames_on(): return lax.ppermute(x, ('dp', 'head'), pairs)  3.84 us
  transfers between devices with their start and end apart: 35, of which 16 were waited for; matrix products, arithmetic and copies ran while one was open for 0% of the time, Pallas kernels for 10%

profile of v1, /device:TPU:1, one launch (start us, length us, event | category | flops | bytes accessed | tf_op | source)
XLA Modules:
  0.0 114.3 jit_solution(10126209817340143596)
XLA Ops:
  0.0 3.3 %collective-permute-start.1 = (bf16[512,768]{1,0:T(8,128)(2,1)}, bf16[512,768]{1,0:T(8,128)(2,1)S(1)}, u32[]{:S(2)}, u32[]{:S(2)}) collective-permute-start(bf16[512,768]{1,0:T(8,128)(2,1)} %refs_0_.3), channel_id=1, source_target_pairs={{0,96},{32,0},{64,32},{96,64},{1,97},{33,1},{65,33},{97,65},{2,98}... | collective-permute-start | bytes 2359304 | tf_op jit(solution)/shard_map/ppermute | solution.py:47
  5.2 7.0 %collective-permute-start.4 = (bf16[192,384]{1,0:T(8,128)(2,1)S(1)}, bf16[192,384]{1,0:T(8,128)(2,1)S(1)}, u32[]{:S(2)}, u32[]{:S(2)}) collective-permute-start(bf16[192,384]{1,0:T(8,128)(2,1)S(1)} %prepare.1), channel_id=1, source_target_pairs={{0,2},{1,3},{2,0},{3,1},{4,6},{5,7},{6,4},{7,5},{8,10},{9,11},{10,... | collective-permute-start | bytes 442376 | tf_op jit(solution)/shard_map/ppermute | solution.py:33
  12.2 2.4 %collective-permute-start.2 = (bf16[192,384]{1,0:T(8,128)(2,1)S(1)}, bf16[192,384]{1,0:T(8,128)(2,1)S(1)}, u32[]{:S(2)}, u32[]{:S(2)}) collective-permute-start(bf16[192,384]{1,0:T(8,128)(2,1)S(1)} %prepare.1), channel_id=1, source_target_pairs={{0,1},{1,2},{2,3},{3,0},{4,5},{5,6},{6,7},{7,4},{8,9},{9,10},{10,1... | collective-permute-start | bytes 442376 | tf_op jit(solution)/shard_map/ppermute | solution.py:33
  14.8 5.4 %collective-permute-done.3 = bf16[192,384]{1,0:T(8,128)(2,1)S(1)} collective-permute-done((bf16[192,384]{1,0:T(8,128)(2,1)S(1)}, bf16[192,384]{1,0:T(8,128)(2,1)S(1)}, u32[]{:S(2)}, u32[]{:S(2)}) %collective-permute-start.3) | collective-permute-done | bytes 147488 | tf_op jit(solution)/shard_map/ppermute | solution.py:33
  20.3 2.5 %collective-permute-start.5 = (bf16[768,384]{1,0:T(8,128)(2,1)S(1)}, bf16[768,384]{1,0:T(8,128)(2,1)S(1)}, u32[]{:S(2)}, u32[]{:S(2)}) collective-permute-start(bf16[768,384]{1,0:T(8,128)(2,1)S(1)} %pad_maximum_fusion.refs_0_.refs_5_), channel_id=1, source_target_pairs={{0,4},{1,5},{2,6},{3,7},{4,8},{5,9},{6,10},{7,11},{8,12},{9,13},{1... | collective-permute-start | bytes 1769480 | tf_op jit(solution)/shard_map/ppermute | solution.py:33
  22.9 6.7 %collective-permute-done.5.refs_1_.refs_6_ = bf16[768,384]{1,0:T(8,128)(2,1)S(1)} collective-permute-done((bf16[768,384]{1,0:T(8,128)(2,1)S(1)}, bf16[768,384]{1,0:T(8,128)(2,1)S(1)}, u32[]{:S(2)}, u32[]{:S(2)}) %collective-permute-start.5) | collective-permute-done | bytes 589856 | tf_op jit(solution)/shard_map/ppermute | solution.py:33
  29.8 2.5 %collective-permute-start.13 = (bf16[256,768]{1,0:T(8,128)(2,1)S(1)}, bf16[256,768]{1,0:T(8,128)(2,1)S(1)}, u32[]{:S(2)}, u32[]{:S(2)}) collective-permute-start(bf16[256,768]{1,0:T(8,128)(2,1)S(1)} %get-tuple-element.37), channel_id=1, source_target_pairs={{0,96},{32,0},{64,32},{96,64},{1,97},{33,1},{65,33},{97,65},{2,98}... | collective-permute-start | bytes 1179656 | tf_op jit(solution)/shard_map/ppermute | solution.py:47
  32.3 2.7 %collective-permute-start.6 = (bf16[768,384]{1,0:T(8,128)(2,1)S(1)}, bf16[768,384]{1,0:T(8,128)(2,1)S(1)}, u32[]{:S(2)}, u32[]{:S(2)}) collective-permute-start(bf16[768,384]{1,0:T(8,128)(2,1)S(1)} %pad_maximum_fusion.refs_0_.refs_5_), channel_id=1, source_target_pairs={{0,28},{1,29},{2,30},{3,31},{4,0},{5,1},{6,2},{7,3},{8,4},{9,5},{1... | collective-permute-start | bytes 1769480 | tf_op jit(solution)/shard_map/ppermute | solution.py:33
  35.9 4.4 %collective-permute-done.11.refs_3_ = bf16[256,768]{1,0:T(8,128)(2,1)S(1)} collective-permute-done((bf16[256,768]{1,0:T(8,128)(2,1)S(1)}, bf16[256,768]{1,0:T(8,128)(2,1)S(1)}, u32[]{:S(2)}, u32[]{:S(2)}) %collective-permute-start.11) | collective-permute-done | bytes 393248 | tf_op jit(solution)/shard_map/ppermute | solution.py:47
  40.3 2.0 %collective-permute-start.12 = (bf16[256,768]{1,0:T(8,128)(2,1)S(1)}, bf16[256,768]{1,0:T(8,128)(2,1)S(1)}, u32[]{:S(2)}, u32[]{:S(2)}) collective-permute-start(bf16[256,768]{1,0:T(8,128)(2,1)S(1)} %collective-permute-done.11.refs_3_), channel_id=1, source_target_pairs={{0,128},{128,0},{1,129},{129,1},{2,130},{130,2},{3,131},{131,3},{4... | collective-permute-start | bytes 1179656 | tf_op jit(solution)/shard_map/ppermute | solution.py:51
  42.3 2.9 %collective-permute-start.16 = (bf16[768,384]{1,0:T(8,128)(2,1)S(1)}, bf16[768,384]{1,0:T(8,128)(2,1)S(1)}, u32[]{:S(2)}, u32[]{:S(2)}) collective-permute-start(bf16[768,384]{1,0:T(8,128)(2,1)S(1)} %collective-permute-done.6.refs_2_.refs_7_), channel_id=1, source_target_pairs={{0,28},{1,29},{2,30},{3,31},{4,0},{5,1},{6,2},{7,3},{8,4},{9,5},{1... | collective-permute-start | bytes 1769480 | tf_op jit(solution)/shard_map/ppermute | solution.py:33
  48.5 3.6 %collective-permute-done.16.refs_4_.refs_9_ = bf16[768,384]{1,0:T(8,128)(2,1)S(1)} collective-permute-done((bf16[768,384]{1,0:T(8,128)(2,1)S(1)}, bf16[768,384]{1,0:T(8,128)(2,1)S(1)}, u32[]{:S(2)}, u32[]{:S(2)}) %collective-permute-start.16) | collective-permute-done | bytes 589856 | tf_op jit(solution)/shard_map/ppermute | solution.py:33
  52.1 3.4 %collective-permute-done.15.refs_5_.refs_10_ = bf16[768,384]{1,0:T(8,128)(2,1)S(1)} collective-permute-done((bf16[768,384]{1,0:T(8,128)(2,1)S(1)}, bf16[768,384]{1,0:T(8,128)(2,1)S(1)}, u32[]{:S(2)}, u32[]{:S(2)}) %collective-permute-start.15) | collective-permute-done | bytes 589856 | tf_op jit(solution)/shard_map/ppermute | solution.py:33
  56.9 7.6 %collective-permute-done.17.refs_6_.refs_11_ = bf16[768,384]{1,0:T(8,128)(2,1)S(1)} collective-permute-done((bf16[768,384]{1,0:T(8,128)(2,1)S(1)}, bf16[768,384]{1,0:T(8,128)(2,1)S(1)}, u32[]{:S(2)}, u32[]{:S(2)}) %collective-permute-start.17) | collective-permute-done | bytes 589856 | tf_op jit(solution)/shard_map/ppermute | solution.py:33
  65.9 3.6 %collective-permute-start.20 = (bf16[1536,384]{1,0:T(8,128)(2,1)S(1)}, bf16[1536,384]{1,0:T(8,128)(2,1)S(1)}, u32[]{:S(2)}, u32[]{:S(2)}) collective-permute-start(bf16[1536,384]{1,0:T(8,128)(2,1)S(1)} %query_half.1.w_own), channel_id=1, source_target_pairs={{0,128},{128,0},{1,129},{129,1},{2,130},{130,2},{3,131},{131,3},{4... | collective-permute-start | bytes 3538952 | tf_op jit(solution)/shard_map/ppermute | solution.py:51
  69.5 2.2 %project_cross.1 = (bf16[512,256]{1,0:T(8,128)(2,1)S(1)}, bf16[512,128]{1,0:T(8,128)(2,1)S(1)}, bf16[3072,384]{1,0:T(8,128)(2,1)S(1)}) custom-call(f32[2,128]{1,0:T(2,128)S(1)} %copy-done.1, bf16[512,768]{1,0:T(8,128)(2,1)S(1)} %collective-permute-done.8.refs_0_, bf16[512,768]{1,0:T(8,128)(2,1)S(1)} %collective-permute-done.9.refs_1_, ...), custom_call_target="tpu_custom_call" | custom-call | flops 1207959552 | bytes 6291456 | tf_op jit(solution)/shard_map/project_cross/pallas_call | solution.py:118
  74.3 1.9 %project_same.1 = (bf16[512,256]{1,0:T(8,128)(2,1)S(1)}, bf16[512,128]{1,0:T(8,128)(2,1)S(1)}) custom-call(f32[2,128]{1,0:T(2,128)S(1)} %copy-done.1, bf16[512,768]{1,0:T(8,128)(2,1)S(1)} %copy-done, bf16[512,768]{1,0:T(8,128)(2,1)S(1)} %collective-permute-done.below.refs_1_, bf16[512,768]{1,0:T(8,128)(2,1)S(1)} %collective-permute-done.1.above.refs_2_, ...), custom_call_target="tpu_custom_call" | custom-call | flops 1207959552 | bytes 6291456 | tf_op jit(solution)/shard_map/project_same/pallas_call | solution.py:118
  76.3 3.7 %collective-permute-start.25 = (bf16[512,256]{1,0:T(8,128)(2,1)S(1)}, bf16[512,256]{1,0:T(8,128)(2,1)S(1)}, u32[]{:S(2)}, u32[]{:S(2)}) collective-permute-start(bf16[512,256]{1,0:T(8,128)(2,1)S(1)} %get-tuple-element.50.refs_0_), channel_id=1, source_target_pairs={{0,31},{1,0},{2,1},{3,2},{4,3},{5,4},{6,5},{7,6},{8,7},{9,8},{10,9... | collective-permute-start | bytes 786440 | tf_op jit(solution)/shard_map/ppermute | solution.py:42
  80.0 2.1 %query.1.q_ref = bf16[512,384]{1,0:T(8,128)(2,1)S(1)} custom-call(f32[2,128]{1,0:T(2,128)S(1)} %copy-done.1, bf16[1536,384]{1,0:T(8,128)(2,1)S(1)} %query_half.1.w_own, bf16[1536,384]{1,0:T(8,128)(2,1)S(1)} %collective-permute-done.20.w_other, bf16[512,768]{1,0:T(8,128)(2,1)S(1)} %copy-done, bf16[512,768]{1,0:T(8,128)(2,1)S(1)} %collective-permute-done.below.refs_1_, ...), custom_call_target="tpu_custom_call" | custom-call | flops 34359738368 | bytes 6291456 | tf_op jit(solution)/shard_map/query/pallas_call | solution.py:118
  82.2 4.9 %collective-permute-start.31 = (bf16[512,256]{1,0:T(8,128)(2,1)S(1)}, bf16[512,256]{1,0:T(8,128)(2,1)S(1)}, u32[]{:S(2)}, u32[]{:S(2)}) collective-permute-start(bf16[512,256]{1,0:T(8,128)(2,1)S(1)} %pack.1), channel_id=1, source_target_pairs={{0,31},{1,0},{2,1},{3,2},{4,3},{5,4},{6,5},{7,6},{8,7},{9,8},{10,9... | collective-permute-start | bytes 786440 | tf_op jit(solution)/shard_map/ppermute | solution.py:42
  88.2 2.2 %collective-permute-done.23.refs_0_ = bf16[512,256]{1,0:T(8,128)(2,1)S(1)} collective-permute-done((bf16[512,256]{1,0:T(8,128)(2,1)S(1)}, bf16[512,256]{1,0:T(8,128)(2,1)S(1)}, u32[]{:S(2)}, u32[]{:S(2)}) %collective-permute-start.23) | collective-permute-done | bytes 262176 | tf_op jit(solution)/shard_map/ppermute | solution.py:42
  91.8 2.0 %collective-permute-start.29 = (bf16[512,256]{1,0:T(8,128)(2,1)S(1)}, bf16[512,256]{1,0:T(8,128)(2,1)S(1)}, u32[]{:S(2)}, u32[]{:S(2)}) collective-permute-start(bf16[512,256]{1,0:T(8,128)(2,1)S(1)} %attend_0.1.refs_0_), channel_id=1, source_target_pairs={{0,64},{32,96},{64,0},{96,32},{1,65},{33,97},{65,1},{97,33},{2,66}... | collective-permute-start | bytes 786440 | tf_op jit(solution)/shard_map/ppermute | solution.py:47
  97.7 2.0 %collective-permute-start.34 = (bf16[512,128]{1,0:T(8,128)(2,1)S(1)}, bf16[512,128]{1,0:T(8,128)(2,1)S(1)}, u32[]{:S(2)}, u32[]{:S(2)}) collective-permute-start(bf16[512,128]{1,0:T(8,128)(2,1)S(1)} %attend_1.1.refs_0_), channel_id=1, source_target_pairs={{0,64},{32,96},{64,0},{96,32},{1,65},{33,97},{65,1},{97,33},{2,66}... | collective-permute-start | bytes 393224 | tf_op jit(solution)/shard_map/ppermute | solution.py:47
  101.2 5.7 %collective-permute-done.28.refs_2_ = bf16[512,256]{1,0:T(8,128)(2,1)S(1)} collective-permute-done((bf16[512,256]{1,0:T(8,128)(2,1)S(1)}, bf16[512,256]{1,0:T(8,128)(2,1)S(1)}, u32[]{:S(2)}, u32[]{:S(2)}) %collective-permute-start.28) | collective-permute-done | bytes 262176 | tf_op jit(solution)/shard_map/ppermute | solution.py:47
  (70 shorter events, 27.5 us)
Async XLA Ops:
  0.0 22.8 %collective-permute-start.1 = (bf16[512,768]{1,0:T(8,128)(2,1)}, bf16[512,768]{1,0:T(8,128)(2,1)S(1)}, u32[]{:S(2)}, u32[]{:S(2)}) collective-permute-start(bf16[512,768]{1,0:T(8,128)(2,1)} %refs_0_.3), channel_id=1, source_target_pairs={{0,96},{32,0},{64,32},{96,64},{1,97},{33,1},{65,33},{97,65},{2,98}... | collective-permute-start | bytes 2359304 | tf_op jit(solution)/shard_map/ppermute | solution.py:47
  3.3 19.5 %collective-permute-start = (bf16[512,768]{1,0:T(8,128)(2,1)}, bf16[512,768]{1,0:T(8,128)(2,1)S(1)}, u32[]{:S(2)}, u32[]{:S(2)}) collective-permute-start(bf16[512,768]{1,0:T(8,128)(2,1)} %refs_0_.3), channel_id=1, source_target_pairs={{0,32},{32,64},{64,96},{96,0},{1,33},{33,65},{65,97},{97,1},{2,34}... | collective-permute-start | bytes 2359304 | tf_op jit(solution)/shard_map/ppermute | solution.py:47
  14.8 20.2 %collective-permute-start.8 = (bf16[512,768]{1,0:T(8,128)(2,1)S(1)}, bf16[512,768]{1,0:T(8,128)(2,1)S(1)}, u32[]{:S(2)}, u32[]{:S(2)}) collective-permute-start(bf16[512,768]{1,0:T(8,128)(2,1)S(1)} %copy-done), channel_id=1, source_target_pairs={{0,128},{128,0},{1,129},{129,1},{2,130},{130,2},{3,131},{131,3},{4... | collective-permute-start | bytes 2359304 | tf_op jit(solution)/shard_map/ppermute | solution.py:51
  29.6 10.7 %collective-permute-start.11 = (bf16[256,768]{1,0:T(8,128)(2,1)S(1)}, bf16[256,768]{1,0:T(8,128)(2,1)S(1)}, u32[]{:S(2)}, u32[]{:S(2)}) collective-permute-start(bf16[256,768]{1,0:T(8,128)(2,1)S(1)} %get-tuple-element.36), channel_id=1, source_target_pairs={{0,32},{32,64},{64,96},{96,0},{1,33},{33,65},{65,97},{97,1},{2,34}... | collective-permute-start | bytes 1179656 | tf_op jit(solution)/shard_map/ppermute | solution.py:47
  29.8 12.5 %collective-permute-start.13 = (bf16[256,768]{1,0:T(8,128)(2,1)S(1)}, bf16[256,768]{1,0:T(8,128)(2,1)S(1)}, u32[]{:S(2)}, u32[]{:S(2)}) collective-permute-start(bf16[256,768]{1,0:T(8,128)(2,1)S(1)} %get-tuple-element.37), channel_id=1, source_target_pairs={{0,96},{32,0},{64,32},{96,64},{1,97},{33,1},{65,33},{97,65},{2,98}... | collective-permute-start | bytes 1179656 | tf_op jit(solution)/shard_map/ppermute | solution.py:47
  32.3 10.1 %collective-permute-start.6 = (bf16[768,384]{1,0:T(8,128)(2,1)S(1)}, bf16[768,384]{1,0:T(8,128)(2,1)S(1)}, u32[]{:S(2)}, u32[]{:S(2)}) collective-permute-start(bf16[768,384]{1,0:T(8,128)(2,1)S(1)} %pad_maximum_fusion.refs_0_.refs_5_), channel_id=1, source_target_pairs={{0,28},{1,29},{2,30},{3,31},{4,0},{5,1},{6,2},{7,3},{8,4},{9,5},{1... | collective-permute-start | bytes 1769480 | tf_op jit(solution)/shard_map/ppermute | solution.py:33
  35.0 10.2 %collective-permute-start.7 = (bf16[768,384]{1,0:T(8,128)(2,1)S(1)}, bf16[768,384]{1,0:T(8,128)(2,1)S(1)}, u32[]{:S(2)}, u32[]{:S(2)}) collective-permute-start(bf16[768,384]{1,0:T(8,128)(2,1)S(1)} %collective-permute-done.5.refs_1_.refs_6_), channel_id=1, source_target_pairs={{0,4},{1,5},{2,6},{3,7},{4,8},{5,9},{6,10},{7,11},{8,12},{9,13},{1... | collective-permute-start | bytes 1769480 | tf_op jit(solution)/shard_map/ppermute | solution.py:33
  35.0 13.5 %collective-permute-start.9 = (bf16[512,768]{1,0:T(8,128)(2,1)S(1)}, bf16[512,768]{1,0:T(8,128)(2,1)S(1)}, u32[]{:S(2)}, u32[]{:S(2)}) collective-permute-start(bf16[512,768]{1,0:T(8,128)(2,1)S(1)} %collective-permute-done.below.refs_1_), channel_id=1, source_target_pairs={{0,128},{128,0},{1,129},{129,1},{2,130},{130,2},{3,131},{131,3},{4... | collective-permute-start | bytes 2359304 | tf_op jit(solution)/shard_map/ppermute | solution.py:51
  42.3 9.7 %collective-permute-start.16 = (bf16[768,384]{1,0:T(8,128)(2,1)S(1)}, bf16[768,384]{1,0:T(8,128)(2,1)S(1)}, u32[]{:S(2)}, u32[]{:S(2)}) collective-permute-start(bf16[768,384]{1,0:T(8,128)(2,1)S(1)} %collective-permute-done.6.refs_2_.refs_7_), channel_id=1, source_target_pairs={{0,28},{1,29},{2,30},{3,31},{4,0},{5,1},{6,2},{7,3},{8,4},{9,5},{1... | collective-permute-start | bytes 1769480 | tf_op jit(solution)/shard_map/ppermute | solution.py:33
  45.2 10.2 %collective-permute-start.15 = (bf16[768,384]{1,0:T(8,128)(2,1)S(1)}, bf16[768,384]{1,0:T(8,128)(2,1)S(1)}, u32[]{:S(2)}, u32[]{:S(2)}) collective-permute-start(bf16[768,384]{1,0:T(8,128)(2,1)S(1)} %collective-permute-done.7.refs_3_.refs_8_), channel_id=1, source_target_pairs={{0,4},{1,5},{2,6},{3,7},{4,8},{5,9},{6,10},{7,11},{8,12},{9,13},{1... | collective-permute-start | bytes 1769480 | tf_op jit(solution)/shard_map/ppermute | solution.py:33
  55.5 10.2 %collective-permute-start.18 = (bf16[768,384]{1,0:T(8,128)(2,1)S(1)}, bf16[768,384]{1,0:T(8,128)(2,1)S(1)}, u32[]{:S(2)}, u32[]{:S(2)}) collective-permute-start(bf16[768,384]{1,0:T(8,128)(2,1)S(1)} %collective-permute-done.15.refs_5_.refs_10_), channel_id=1, source_target_pairs={{0,4},{1,5},{2,6},{3,7},{4,8},{5,9},{6,10},{7,11},{8,12},{9,13},{1... | collective-permute-start | bytes 1769480 | tf_op jit(solution)/shard_map/ppermute | solution.py:33
  65.9 14.1 %collective-permute-start.20 = (bf16[1536,384]{1,0:T(8,128)(2,1)S(1)}, bf16[1536,384]{1,0:T(8,128)(2,1)S(1)}, u32[]{:S(2)}, u32[]{:S(2)}) collective-permute-start(bf16[1536,384]{1,0:T(8,128)(2,1)S(1)} %query_half.1.w_own), channel_id=1, source_target_pairs={{0,128},{128,0},{1,129},{129,1},{2,130},{130,2},{3,131},{131,3},{4... | collective-permute-start | bytes 3538952 | tf_op jit(solution)/shard_map/ppermute | solution.py:51
  72.2 9.9 %collective-permute-start.26 = (bf16[512,256]{1,0:T(8,128)(2,1)S(1)}, bf16[512,256]{1,0:T(8,128)(2,1)S(1)}, u32[]{:S(2)}, u32[]{:S(2)}) collective-permute-start(bf16[512,256]{1,0:T(8,128)(2,1)S(1)} %get-tuple-element.46), channel_id=1, source_target_pairs={{0,159},{1,128},{2,129},{3,130},{4,131},{5,132},{6,133},{7,134},{8... | collective-permute-start | bytes 786440 | tf_op jit(solution)/shard_map/ppermute | solution.py:42
  72.5 14.6 %collective-permute-start.24 = (bf16[512,256]{1,0:T(8,128)(2,1)S(1)}, bf16[512,256]{1,0:T(8,128)(2,1)S(1)}, u32[]{:S(2)}, u32[]{:S(2)}) collective-permute-start(bf16[512,256]{1,0:T(8,128)(2,1)S(1)} %get-tuple-element.46), channel_id=1, source_target_pairs={{0,129},{1,130},{2,131},{3,132},{4,133},{5,134},{6,135},{7,136},{8... | collective-permute-start | bytes 786440 | tf_op jit(solution)/shard_map/ppermute | solution.py:42
  74.2 25.6 %collective-permute-start.19 = (bf16[1536,384]{1,0:T(8,128)(2,1)S(1)}, bf16[1536,384]{1,0:T(8,128)(2,1)S(1)}, u32[]{:S(2)}, u32[]{:S(2)}) collective-permute-start(bf16[1536,384]{1,0:T(8,128)(2,1)S(1)} %out_half.1.w_own), channel_id=1, source_target_pairs={{0,128},{128,0},{1,129},{129,1},{2,130},{130,2},{3,131},{131,3},{4... | collective-permute-start | bytes 3538952 | tf_op jit(solution)/shard_map/ppermute | solution.py:51
  76.3 11.9 %collective-permute-start.25 = (bf16[512,256]{1,0:T(8,128)(2,1)S(1)}, bf16[512,256]{1,0:T(8,128)(2,1)S(1)}, u32[]{:S(2)}, u32[]{:S(2)}) collective-permute-start(bf16[512,256]{1,0:T(8,128)(2,1)S(1)} %get-tuple-element.50.refs_0_), channel_id=1, source_target_pairs={{0,31},{1,0},{2,1},{3,2},{4,3},{5,4},{6,5},{7,6},{8,7},{9,8},{10,9... | collective-permute-start | bytes 786440 | tf_op jit(solution)/shard_map/ppermute | solution.py:42
  80.0 10.5 %collective-permute-start.23 = (bf16[512,256]{1,0:T(8,128)(2,1)S(1)}, bf16[512,256]{1,0:T(8,128)(2,1)S(1)}, u32[]{:S(2)}, u32[]{:S(2)}) collective-permute-start(bf16[512,256]{1,0:T(8,128)(2,1)S(1)} %get-tuple-element.50.refs_0_), channel_id=1, source_target_pairs={{0,1},{1,2},{2,3},{3,4},{4,5},{5,6},{6,7},{7,8},{8,9},{9,10},{10,1... | collective-permute-start | bytes 786440 | tf_op jit(solution)/shard_map/ppermute | solution.py:42
  82.2 11.9 %collective-permute-start.31 = (bf16[512,256]{1,0:T(8,128)(2,1)S(1)}, bf16[512,256]{1,0:T(8,128)(2,1)S(1)}, u32[]{:S(2)}, u32[]{:S(2)}) collective-permute-start(bf16[512,256]{1,0:T(8,128)(2,1)S(1)} %pack.1), channel_id=1, source_target_pairs={{0,31},{1,0},{2,1},{3,2},{4,3},{5,4},{6,5},{7,6},{8,7},{9,8},{10,9... | collective-permute-start | bytes 786440 | tf_op jit(solution)/shard_map/ppermute | solution.py:42
  87.1 9.9 %collective-permute-start.30 = (bf16[512,256]{1,0:T(8,128)(2,1)S(1)}, bf16[512,256]{1,0:T(8,128)(2,1)S(1)}, u32[]{:S(2)}, u32[]{:S(2)}) collective-permute-start(bf16[512,256]{1,0:T(8,128)(2,1)S(1)} %pack.1), channel_id=1, source_target_pairs={{0,1},{1,2},{2,3},{3,4},{4,5},{5,6},{6,7},{7,8},{8,9},{9,10},{10,1... | collective-permute-start | bytes 786440 | tf_op jit(solution)/shard_map/ppermute | solution.py:42
  93.9 13.0 %collective-permute-start.28 = (bf16[512,256]{1,0:T(8,128)(2,1)S(1)}, bf16[512,256]{1,0:T(8,128)(2,1)S(1)}, u32[]{:S(2)}, u32[]{:S(2)}) collective-permute-start(bf16[512,256]{1,0:T(8,128)(2,1)S(1)} %attend_0.1.refs_0_), channel_id=1, source_target_pairs={{0,96},{32,0},{64,32},{96,64},{1,97},{33,1},{65,33},{97,65},{2,98}... | collective-permute-start | bytes 786440 | tf_op jit(solution)/shard_map/ppermute | solution.py:47
  94.1 14.1 %collective-permute-start.27 = (bf16[512,256]{1,0:T(8,128)(2,1)S(1)}, bf16[512,256]{1,0:T(8,128)(2,1)S(1)}, u32[]{:S(2)}, u32[]{:S(2)}) collective-permute-start(bf16[512,256]{1,0:T(8,128)(2,1)S(1)} %attend_0.1.refs_0_), channel_id=1, source_target_pairs={{0,32},{32,64},{64,96},{96,0},{1,33},{33,65},{65,97},{97,1},{2,34}... | collective-permute-start | bytes 786440 | tf_op jit(solution)/shard_map/ppermute | solution.py:47
  97.7 11.7 %collective-permute-start.34 = (bf16[512,128]{1,0:T(8,128)(2,1)S(1)}, bf16[512,128]{1,0:T(8,128)(2,1)S(1)}, u32[]{:S(2)}, u32[]{:S(2)}) collective-permute-start(bf16[512,128]{1,0:T(8,128)(2,1)S(1)} %attend_1.1.refs_0_), channel_id=1, source_target_pairs={{0,64},{32,96},{64,0},{96,32},{1,65},{33,97},{65,1},{97,33},{2,66}... | collective-permute-start | bytes 393224 | tf_op jit(solution)/shard_map/ppermute | solution.py:47
  99.7 11.4 %collective-permute-start.33 = (bf16[512,128]{1,0:T(8,128)(2,1)S(1)}, bf16[512,128]{1,0:T(8,128)(2,1)S(1)}, u32[]{:S(2)}, u32[]{:S(2)}) collective-permute-start(bf16[512,128]{1,0:T(8,128)(2,1)S(1)} %attend_1.1.refs_0_), channel_id=1, source_target_pairs={{0,96},{32,0},{64,32},{96,64},{1,97},{33,1},{65,33},{97,65},{2,98}... | collective-permute-start | bytes 393224 | tf_op jit(solution)/shard_map/ppermute | solution.py:47
  100.0 12.4 %collective-permute-start.32 = (bf16[512,128]{1,0:T(8,128)(2,1)S(1)}, bf16[512,128]{1,0:T(8,128)(2,1)S(1)}, u32[]{:S(2)}, u32[]{:S(2)}) collective-permute-start(bf16[512,128]{1,0:T(8,128)(2,1)S(1)} %attend_1.1.refs_0_), channel_id=1, source_target_pairs={{0,32},{32,64},{64,96},{96,0},{1,33},{33,65},{65,97},{97,1},{2,34}... | collective-permute-start | bytes 393224 | tf_op jit(solution)/shard_map/ppermute | solution.py:47
  (16 other events, 133.7 us)

commit v2 on v1

--- a/solution.py
+++ b/solution.py
@@ -79,8 +79,8 @@
     p3, p2 = moved(p1, (1, 0), (0, 1)), moved(s, (-1, 0), (0, -1))
     p5, p4 = moved(p3, (1, 0), (0, 1)), moved(p2, (-1, 0), (0, -1))
     pieces = (tokens, below, above, far_top, far_bottom)
-    others = tuple(swapped(x) for x in pieces)
-    *others, p5, p4 = lax.optimization_barrier((*others, p5, p4))
+    others = [swapped(x) for x in pieces]
+    *others[3:], p5, p4 = lax.optimization_barrier((*others[3:], p5, p4))
     p7, p6 = moved(p5, (1, 0), (0, 1)), moved(p4, (-1, 0), (0, -1))
     return pieces, others, (s, p1, p2, p3, p4, p5, p6, p7)
 
@@ -298,32 +298,25 @@
     core, seq = lax.axis_index("dp"), lax.axis_index("seq")
     width, cols = w_own.shape[0] // NX, w_own.shape[1]
     size = len(group) * HD
+    pairs = [
+        (jnp.concatenate([pieces[i][...], pieces[j][...]], axis=1), (steps_i, steps_j))
+        for (i, steps_i), (j, steps_j) in (((0, 0), (1, 3)), ((2, 1), (3, 2)))
+    ]
     for w, side in ((w_own, core), (w_other, 1 - core)):
         to = pl.ds(pl.multiple_of(side * cols, HD), cols)
-
-        def part(ref, step, w=w):
-            at = pl.multiple_of(lax.rem(seq + step, NX) * width + group[0] * HD, HD)
-            return jnp.dot(ref[...], w[pl.ds(at, size), :], preferred_element_type=F32)
-
-        near = part(pieces[0], 0) + part(pieces[1], 3) + part(pieces[2], 1)
-        if total is not None:
-            near = near + total[:, to]
-        start = 0
-        for far in pieces[3:]:
-            rows = slice(start, start + far.shape[0])
-            out[rows, to] = (near[rows] + part(far, 2)).astype(out.dtype)
-            start += far.shape[0]
+        product = None if total is None else total[:, to]
+        for x, steps in pairs:
+            rows = []
+            for step in steps:
+                at = pl.multiple_of(lax.rem(seq + step, NX) * width + group[0] * HD, HD)
+                rows.append(w[pl.ds(at, size), :])
+            part = jnp.dot(x, jnp.concatenate(rows, axis=0), preferred_element_type=F32)
+            product = part if product is None else product + part
+        out[:, to] = product.astype(out.dtype)
 
 
 def first_kernel(group, w_own, w_other, *refs):
     output_kernel(group, w_own, w_other, None, *refs)
-
-
-def ring_x(x):
-    half = x.shape[0] // 2
-    below = along(x, "seq", 1)
-    above = along(x, "seq", -1)
-    return x, below, above, along(below[:half], "seq", 1), along(above[half:], "seq", -1)
 
 
 def direct_x(x):

time: 114 us -> 111 us (0.974)
  waiting for transfers between devices: 47.7 us -> 44.7 us
    ppermute x10, waiting for transfers between devices: 14.4 us -> 11 us  [along(): return lax.ppermute(x, axis, [(i, (i + step) % n) for i in range(n)])]
  transfers between devices with their start and end apart: 35 -> 35, of which waited for: 16 -> 18; matrix products, arithmetic and copies ran while one was open for 0% -> 0% of each run, Pallas kernels for 10% -> 10%
where the time goes in v2:
time: 111 us
  starting transfers between devices  51 us (46%)
  waiting for transfers between devices  44.7 us (40%)
  Pallas kernels  12.9 us (12%)
  local copies, waits for them, and re-layouts  1.84 us (2%)
    ppermute x10, waiting for transfers between devices, moved(): return lax.ppermute(x, ('dp', 'head'), pairs)  28 us
    ppermute x10, starting transfers between devices, moved(): return lax.ppermute(x, ('dp', 'head'), pairs)  19.5 us
    ppermute x10, starting transfers between devices, along(): return lax.ppermute(x, axis, [(i, (i + step) % n) for i in range(n)])  13.1 us
    pallas_call x13, Pallas kernels, call(): pl.pallas_call(kernel, out_shape=out_shape, in_specs=[VMEM] * n, out_spec...  12.9 us
    ppermute x10, waiting for transfers between devices, along(): return lax.ppermute(x, axis, [(i, (i + step) % n) for i in range(n)])  11 us
    ppermute x6, starting transfers between devices, frames_on(): return lax.ppermute(x, ('dp', 'head'), pairs)  10.3 us
    ppermute x9, starting transfers between devices, swapped(): return lax.ppermute(x, 'dp', [(0, 1), (1, 0)])  8.16 us
    ppermute x6, waiting for transfers between devices, frames_on(): return lax.ppermute(x, ('dp', 'head'), pairs)  3.8 us
  transfers between devices with their start and end apart: 35, of which 18 were waited for; matrix products, arithmetic and copies ran while one was open for 0% of the time, Pallas kernels for 10%

profile of v2, /device:TPU:1, one launch (start us, length us, event | category | flops | bytes accessed | tf_op | source)
XLA Modules:
  0.0 110.6 jit_solution(754584443055524099)
XLA Ops:
  0.0 3.3 %collective-permute-start.1 = (bf16[512,768]{1,0:T(8,128)(2,1)}, bf16[512,768]{1,0:T(8,128)(2,1)S(1)}, u32[]{:S(2)}, u32[]{:S(2)}) collective-permute-start(bf16[512,768]{1,0:T(8,128)(2,1)} %refs_0_.3), channel_id=1, source_target_pairs={{0,96},{32,0},{64,32},{96,64},{1,97},{33,1},{65,33},{97,65},{2,98}... | collective-permute-start | bytes 2359304 | tf_op jit(solution)/shard_map/ppermute | solution.py:47
  5.2 7.0 %collective-permute-start.4 = (bf16[192,384]{1,0:T(8,128)(2,1)S(1)}, bf16[192,384]{1,0:T(8,128)(2,1)S(1)}, u32[]{:S(2)}, u32[]{:S(2)}) collective-permute-start(bf16[192,384]{1,0:T(8,128)(2,1)S(1)} %prepare.1), channel_id=1, source_target_pairs={{0,2},{1,3},{2,0},{3,1},{4,6},{5,7},{6,4},{7,5},{8,10},{9,11},{10,... | collective-permute-start | bytes 442376 | tf_op jit(solution)/shard_map/ppermute | solution.py:33
  12.2 2.4 %collective-permute-start.2 = (bf16[192,384]{1,0:T(8,128)(2,1)S(1)}, bf16[192,384]{1,0:T(8,128)(2,1)S(1)}, u32[]{:S(2)}, u32[]{:S(2)}) collective-permute-start(bf16[192,384]{1,0:T(8,128)(2,1)S(1)} %prepare.1), channel_id=1, source_target_pairs={{0,1},{1,2},{2,3},{3,0},{4,5},{5,6},{6,7},{7,4},{8,9},{9,10},{10,1... | collective-permute-start | bytes 442376 | tf_op jit(solution)/shard_map/ppermute | solution.py:33
  14.8 5.4 %collective-permute-done.3 = bf16[192,384]{1,0:T(8,128)(2,1)S(1)} collective-permute-done((bf16[192,384]{1,0:T(8,128)(2,1)S(1)}, bf16[192,384]{1,0:T(8,128)(2,1)S(1)}, u32[]{:S(2)}, u32[]{:S(2)}) %collective-permute-start.3) | collective-permute-done | bytes 147488 | tf_op jit(solution)/shard_map/ppermute | solution.py:33
  20.3 2.5 %collective-permute-start.5 = (bf16[768,384]{1,0:T(8,128)(2,1)S(1)}, bf16[768,384]{1,0:T(8,128)(2,1)S(1)}, u32[]{:S(2)}, u32[]{:S(2)}) collective-permute-start(bf16[768,384]{1,0:T(8,128)(2,1)S(1)} %pad_maximum_fusion.refs_0_.refs_5_), channel_id=1, source_target_pairs={{0,4},{1,5},{2,6},{3,7},{4,8},{5,9},{6,10},{7,11},{8,12},{9,13},{1... | collective-permute-start | bytes 1769480 | tf_op jit(solution)/shard_map/ppermute | solution.py:33
  22.9 6.7 %collective-permute-done.5.refs_1_.refs_6_ = bf16[768,384]{1,0:T(8,128)(2,1)S(1)} collective-permute-done((bf16[768,384]{1,0:T(8,128)(2,1)S(1)}, bf16[768,384]{1,0:T(8,128)(2,1)S(1)}, u32[]{:S(2)}, u32[]{:S(2)}) %collective-permute-start.5) | collective-permute-done | bytes 589856 | tf_op jit(solution)/shard_map/ppermute | solution.py:33
  29.6 2.7 %collective-permute-start.6 = (bf16[768,384]{1,0:T(8,128)(2,1)S(1)}, bf16[768,384]{1,0:T(8,128)(2,1)S(1)}, u32[]{:S(2)}, u32[]{:S(2)}) collective-permute-start(bf16[768,384]{1,0:T(8,128)(2,1)S(1)} %pad_maximum_fusion.refs_0_.refs_5_), channel_id=1, source_target_pairs={{0,28},{1,29},{2,30},{3,31},{4,0},{5,1},{6,2},{7,3},{8,4},{9,5},{1... | collective-permute-start | bytes 1769480 | tf_op jit(solution)/shard_map/ppermute | solution.py:33
  32.5 2.5 %collective-permute-start.10 = (bf16[256,768]{1,0:T(8,128)(2,1)S(1)}, bf16[256,768]{1,0:T(8,128)(2,1)S(1)}, u32[]{:S(2)}, u32[]{:S(2)}) collective-permute-start(bf16[256,768]{1,0:T(8,128)(2,1)S(1)} %get-tuple-element.32), channel_id=1, source_target_pairs={{0,96},{32,0},{64,32},{96,64},{1,97},{33,1},{65,33},{97,65},{2,98}... | collective-permute-start | bytes 1179656 | tf_op jit(solution)/shard_map/ppermute | solution.py:47
  35.0 4.1 %collective-permute-done.6.refs_2_.refs_7_ = bf16[768,384]{1,0:T(8,128)(2,1)S(1)} collective-permute-done((bf16[768,384]{1,0:T(8,128)(2,1)S(1)}, bf16[768,384]{1,0:T(8,128)(2,1)S(1)}, u32[]{:S(2)}, u32[]{:S(2)}) %collective-permute-start.6) | collective-permute-done | bytes 589856 | tf_op jit(solution)/shard_map/ppermute | solution.py:33
  39.2 3.4 %collective-permute-start.13 = (bf16[768,384]{1,0:T(8,128)(2,1)S(1)}, bf16[768,384]{1,0:T(8,128)(2,1)S(1)}, u32[]{:S(2)}, u32[]{:S(2)}) collective-permute-start(bf16[768,384]{1,0:T(8,128)(2,1)S(1)} %collective-permute-done.6.refs_2_.refs_7_), channel_id=1, source_target_pairs={{0,28},{1,29},{2,30},{3,31},{4,0},{5,1},{6,2},{7,3},{8,4},{9,5},{1... | collective-permute-start | bytes 1769480 | tf_op jit(solution)/shard_map/ppermute | solution.py:33
  47.0 2.4 %collective-permute-done.13.refs_4_.refs_9_ = bf16[768,384]{1,0:T(8,128)(2,1)S(1)} collective-permute-done((bf16[768,384]{1,0:T(8,128)(2,1)S(1)}, bf16[768,384]{1,0:T(8,128)(2,1)S(1)}, u32[]{:S(2)}, u32[]{:S(2)}) %collective-permute-start.13) | collective-permute-done | bytes 589856 | tf_op jit(solution)/shard_map/ppermute | solution.py:33
  49.4 3.4 %collective-permute-done.12.refs_5_.refs_10_ = bf16[768,384]{1,0:T(8,128)(2,1)S(1)} collective-permute-done((bf16[768,384]{1,0:T(8,128)(2,1)S(1)}, bf16[768,384]{1,0:T(8,128)(2,1)S(1)}, u32[]{:S(2)}, u32[]{:S(2)}) %collective-permute-start.12) | collective-permute-done | bytes 589856 | tf_op jit(solution)/shard_map/ppermute | solution.py:33
  54.3 2.6 %collective-permute-start.18 = (bf16[512,768]{1,0:T(8,128)(2,1)S(1)}, bf16[512,768]{1,0:T(8,128)(2,1)S(1)}, u32[]{:S(2)}, u32[]{:S(2)}) collective-permute-start(bf16[512,768]{1,0:T(8,128)(2,1)S(1)} %copy-done), channel_id=1, source_target_pairs={{0,128},{128,0},{1,129},{129,1},{2,130},{130,2},{3,131},{131,3},{4... | collective-permute-start | bytes 2359304 | tf_op jit(solution)/shard_map/ppermute | solution.py:51
  57.4 4.4 %collective-permute-done.14.refs_6_.refs_11_ = bf16[768,384]{1,0:T(8,128)(2,1)S(1)} collective-permute-done((bf16[768,384]{1,0:T(8,128)(2,1)S(1)}, bf16[768,384]{1,0:T(8,128)(2,1)S(1)}, u32[]{:S(2)}, u32[]{:S(2)}) %collective-permute-start.14) | collective-permute-done | bytes 589856 | tf_op jit(solution)/shard_map/ppermute | solution.py:33
  63.2 3.0 %collective-permute-start.17 = (bf16[1536,384]{1,0:T(8,128)(2,1)S(1)}, bf16[1536,384]{1,0:T(8,128)(2,1)S(1)}, u32[]{:S(2)}, u32[]{:S(2)}) collective-permute-start(bf16[1536,384]{1,0:T(8,128)(2,1)S(1)} %query_half.1.w_own), channel_id=1, source_target_pairs={{0,128},{128,0},{1,129},{129,1},{2,130},{130,2},{3,131},{131,3},{4... | collective-permute-start | bytes 3538952 | tf_op jit(solution)/shard_map/ppermute | solution.py:51
  66.2 2.2 %project_cross.1 = (bf16[512,256]{1,0:T(8,128)(2,1)S(1)}, bf16[512,128]{1,0:T(8,128)(2,1)S(1)}, bf16[3072,384]{1,0:T(8,128)(2,1)S(1)}) custom-call(f32[2,128]{1,0:T(2,128)S(1)} %copy-done.1, bf16[512,768]{1,0:T(8,128)(2,1)S(1)} %collective-permute-done.18.refs_0_, bf16[512,768]{1,0:T(8,128)(2,1)S(1)} %collective-permute-done.19.refs_1_, ...), custom_call_target="tpu_custom_call" | custom-call | flops 1207959552 | bytes 6291456 | tf_op jit(solution)/shard_map/project_cross/pallas_call | solution.py:118
  73.1 3.7 %collective-permute-start.25 = (bf16[512,256]{1,0:T(8,128)(2,1)S(1)}, bf16[512,256]{1,0:T(8,128)(2,1)S(1)}, u32[]{:S(2)}, u32[]{:S(2)}) collective-permute-start(bf16[512,256]{1,0:T(8,128)(2,1)S(1)} %get-tuple-element.44.refs_0_), channel_id=1, source_target_pairs={{0,31},{1,0},{2,1},{3,2},{4,3},{5,4},{6,5},{7,6},{8,7},{9,8},{10,9... | collective-permute-start | bytes 786440 | tf_op jit(solution)/shard_map/ppermute | solution.py:42
  76.8 2.1 %query.1.q_ref = bf16[512,384]{1,0:T(8,128)(2,1)S(1)} custom-call(f32[2,128]{1,0:T(2,128)S(1)} %copy-done.1, bf16[1536,384]{1,0:T(8,128)(2,1)S(1)} %query_half.1.w_own, bf16[1536,384]{1,0:T(8,128)(2,1)S(1)} %collective-permute-done.17.w_other, bf16[512,768]{1,0:T(8,128)(2,1)S(1)} %copy-done, bf16[512,768]{1,0:T(8,128)(2,1)S(1)} %collective-permute-done.below.refs_1_, ...), custom_call_target="tpu_custom_call" | custom-call | flops 34359738368 | bytes 6291456 | tf_op jit(solution)/shard_map/query/pallas_call | solution.py:118
  79.0 4.9 %collective-permute-start.31 = (bf16[512,256]{1,0:T(8,128)(2,1)S(1)}, bf16[512,256]{1,0:T(8,128)(2,1)S(1)}, u32[]{:S(2)}, u32[]{:S(2)}) collective-permute-start(bf16[512,256]{1,0:T(8,128)(2,1)S(1)} %pack.1), channel_id=1, source_target_pairs={{0,31},{1,0},{2,1},{3,2},{4,3},{5,4},{6,5},{7,6},{8,7},{9,8},{10,9... | collective-permute-start | bytes 786440 | tf_op jit(solution)/shard_map/ppermute | solution.py:42
  85.0 2.2 %collective-permute-done.23.refs_0_ = bf16[512,256]{1,0:T(8,128)(2,1)S(1)} collective-permute-done((bf16[512,256]{1,0:T(8,128)(2,1)S(1)}, bf16[512,256]{1,0:T(8,128)(2,1)S(1)}, u32[]{:S(2)}, u32[]{:S(2)}) %collective-permute-start.23) | collective-permute-done | bytes 262176 | tf_op jit(solution)/shard_map/ppermute | solution.py:42
  88.6 2.0 %collective-permute-start.29 = (bf16[512,256]{1,0:T(8,128)(2,1)S(1)}, bf16[512,256]{1,0:T(8,128)(2,1)S(1)}, u32[]{:S(2)}, u32[]{:S(2)}) collective-permute-start(bf16[512,256]{1,0:T(8,128)(2,1)S(1)} %attend_0.1.refs_0_), channel_id=1, source_target_pairs={{0,64},{32,96},{64,0},{96,32},{1,65},{33,97},{65,1},{97,33},{2,66}... | collective-permute-start | bytes 786440 | tf_op jit(solution)/shard_map/ppermute | solution.py:47
  94.5 1.9 %collective-permute-start.34 = (bf16[512,128]{1,0:T(8,128)(2,1)S(1)}, bf16[512,128]{1,0:T(8,128)(2,1)S(1)}, u32[]{:S(2)}, u32[]{:S(2)}) collective-permute-start(bf16[512,128]{1,0:T(8,128)(2,1)S(1)} %attend_1.1.refs_0_), channel_id=1, source_target_pairs={{0,64},{32,96},{64,0},{96,32},{1,65},{33,97},{65,1},{97,33},{2,66}... | collective-permute-start | bytes 393224 | tf_op jit(solution)/shard_map/ppermute | solution.py:47
  98.1 5.9 %collective-permute-done.28.refs_2_ = bf16[512,256]{1,0:T(8,128)(2,1)S(1)} collective-permute-done((bf16[512,256]{1,0:T(8,128)(2,1)S(1)}, bf16[512,256]{1,0:T(8,128)(2,1)S(1)}, u32[]{:S(2)}, u32[]{:S(2)}) %collective-permute-start.28) | collective-permute-done | bytes 262176 | tf_op jit(solution)/shard_map/ppermute | solution.py:47
  106.0 2.6 %collective-permute-done.33.refs_2_ = bf16[512,128]{1,0:T(8,128)(2,1)S(1)} collective-permute-done((bf16[512,128]{1,0:T(8,128)(2,1)S(1)}, bf16[512,128]{1,0:T(8,128)(2,1)S(1)}, u32[]{:S(2)}, u32[]{:S(2)}) %collective-permute-start.33) | collective-permute-done | bytes 131104 | tf_op jit(solution)/shard_map/ppermute | solution.py:47
  (70 shorter events, 27.0 us)
Async XLA Ops:
  0.0 22.8 %collective-permute-start.1 = (bf16[512,768]{1,0:T(8,128)(2,1)}, bf16[512,768]{1,0:T(8,128)(2,1)S(1)}, u32[]{:S(2)}, u32[]{:S(2)}) collective-permute-start(bf16[512,768]{1,0:T(8,128)(2,1)} %refs_0_.3), channel_id=1, source_target_pairs={{0,96},{32,0},{64,32},{96,64},{1,97},{33,1},{65,33},{97,65},{2,98}... | collective-permute-start | bytes 2359304 | tf_op jit(solution)/shard_map/ppermute | solution.py:47
  3.3 19.5 %collective-permute-start = (bf16[512,768]{1,0:T(8,128)(2,1)}, bf16[512,768]{1,0:T(8,128)(2,1)S(1)}, u32[]{:S(2)}, u32[]{:S(2)}) collective-permute-start(bf16[512,768]{1,0:T(8,128)(2,1)} %refs_0_.3), channel_id=1, source_target_pairs={{0,32},{32,64},{64,96},{96,0},{1,33},{33,65},{65,97},{97,1},{2,34}... | collective-permute-start | bytes 2359304 | tf_op jit(solution)/shard_map/ppermute | solution.py:47
  5.2 9.6 %collective-permute-start.4 = (bf16[192,384]{1,0:T(8,128)(2,1)S(1)}, bf16[192,384]{1,0:T(8,128)(2,1)S(1)}, u32[]{:S(2)}, u32[]{:S(2)}) collective-permute-start(bf16[192,384]{1,0:T(8,128)(2,1)S(1)} %prepare.1), channel_id=1, source_target_pairs={{0,2},{1,3},{2,0},{3,1},{4,6},{5,7},{6,4},{7,5},{8,10},{9,11},{10,... | collective-permute-start | bytes 442376 | tf_op jit(solution)/shard_map/ppermute | solution.py:33
  29.6 9.6 %collective-permute-start.6 = (bf16[768,384]{1,0:T(8,128)(2,1)S(1)}, bf16[768,384]{1,0:T(8,128)(2,1)S(1)}, u32[]{:S(2)}, u32[]{:S(2)}) collective-permute-start(bf16[768,384]{1,0:T(8,128)(2,1)S(1)} %pad_maximum_fusion.refs_0_.refs_5_), channel_id=1, source_target_pairs={{0,28},{1,29},{2,30},{3,31},{4,0},{5,1},{6,2},{7,3},{8,4},{9,5},{1... | collective-permute-start | bytes 1769480 | tf_op jit(solution)/shard_map/ppermute | solution.py:33
  32.3 10.2 %collective-permute-start.7 = (bf16[768,384]{1,0:T(8,128)(2,1)S(1)}, bf16[768,384]{1,0:T(8,128)(2,1)S(1)}, u32[]{:S(2)}, u32[]{:S(2)}) collective-permute-start(bf16[768,384]{1,0:T(8,128)(2,1)S(1)} %collective-permute-done.5.refs_1_.refs_6_), channel_id=1, source_target_pairs={{0,4},{1,5},{2,6},{3,7},{4,8},{5,9},{6,10},{7,11},{8,12},{9,13},{1... | collective-permute-start | bytes 1769480 | tf_op jit(solution)/shard_map/ppermute | solution.py:33
  32.3 11.5 %collective-permute-start.8 = (bf16[256,768]{1,0:T(8,128)(2,1)S(1)}, bf16[256,768]{1,0:T(8,128)(2,1)S(1)}, u32[]{:S(2)}, u32[]{:S(2)}) collective-permute-start(bf16[256,768]{1,0:T(8,128)(2,1)S(1)} %get-tuple-element.31), channel_id=1, source_target_pairs={{0,32},{32,64},{64,96},{96,0},{1,33},{33,65},{65,97},{97,1},{2,34}... | collective-permute-start | bytes 1179656 | tf_op jit(solution)/shard_map/ppermute | solution.py:47
  32.5 12.5 %collective-permute-start.10 = (bf16[256,768]{1,0:T(8,128)(2,1)S(1)}, bf16[256,768]{1,0:T(8,128)(2,1)S(1)}, u32[]{:S(2)}, u32[]{:S(2)}) collective-permute-start(bf16[256,768]{1,0:T(8,128)(2,1)S(1)} %get-tuple-element.32), channel_id=1, source_target_pairs={{0,96},{32,0},{64,32},{96,64},{1,97},{33,1},{65,33},{97,65},{2,98}... | collective-permute-start | bytes 1179656 | tf_op jit(solution)/shard_map/ppermute | solution.py:47
  39.2 10.2 %collective-permute-start.13 = (bf16[768,384]{1,0:T(8,128)(2,1)S(1)}, bf16[768,384]{1,0:T(8,128)(2,1)S(1)}, u32[]{:S(2)}, u32[]{:S(2)}) collective-permute-start(bf16[768,384]{1,0:T(8,128)(2,1)S(1)} %collective-permute-done.6.refs_2_.refs_7_), channel_id=1, source_target_pairs={{0,28},{1,29},{2,30},{3,31},{4,0},{5,1},{6,2},{7,3},{8,4},{9,5},{1... | collective-permute-start | bytes 1769480 | tf_op jit(solution)/shard_map/ppermute | solution.py:33
  42.6 10.2 %collective-permute-start.12 = (bf16[768,384]{1,0:T(8,128)(2,1)S(1)}, bf16[768,384]{1,0:T(8,128)(2,1)S(1)}, u32[]{:S(2)}, u32[]{:S(2)}) collective-permute-start(bf16[768,384]{1,0:T(8,128)(2,1)S(1)} %collective-permute-done.7.refs_3_.refs_8_), channel_id=1, source_target_pairs={{0,4},{1,5},{2,6},{3,7},{4,8},{5,9},{6,10},{7,11},{8,12},{9,13},{1... | collective-permute-start | bytes 1769480 | tf_op jit(solution)/shard_map/ppermute | solution.py:33
  52.8 10.2 %collective-permute-start.15 = (bf16[768,384]{1,0:T(8,128)(2,1)S(1)}, bf16[768,384]{1,0:T(8,128)(2,1)S(1)}, u32[]{:S(2)}, u32[]{:S(2)}) collective-permute-start(bf16[768,384]{1,0:T(8,128)(2,1)S(1)} %collective-permute-done.12.refs_5_.refs_10_), channel_id=1, source_target_pairs={{0,4},{1,5},{2,6},{3,7},{4,8},{5,9},{6,10},{7,11},{8,12},{9,13},{1... | collective-permute-start | bytes 1769480 | tf_op jit(solution)/shard_map/ppermute | solution.py:33
  54.3 11.9 %collective-permute-start.18 = (bf16[512,768]{1,0:T(8,128)(2,1)S(1)}, bf16[512,768]{1,0:T(8,128)(2,1)S(1)}, u32[]{:S(2)}, u32[]{:S(2)}) collective-permute-start(bf16[512,768]{1,0:T(8,128)(2,1)S(1)} %copy-done), channel_id=1, source_target_pairs={{0,128},{128,0},{1,129},{129,1},{2,130},{130,2},{3,131},{131,3},{4... | collective-permute-start | bytes 2359304 | tf_op jit(solution)/shard_map/ppermute | solution.py:51
  63.2 13.6 %collective-permute-start.17 = (bf16[1536,384]{1,0:T(8,128)(2,1)S(1)}, bf16[1536,384]{1,0:T(8,128)(2,1)S(1)}, u32[]{:S(2)}, u32[]{:S(2)}) collective-permute-start(bf16[1536,384]{1,0:T(8,128)(2,1)S(1)} %query_half.1.w_own), channel_id=1, source_target_pairs={{0,128},{128,0},{1,129},{129,1},{2,130},{130,2},{3,131},{131,3},{4... | collective-permute-start | bytes 3538952 | tf_op jit(solution)/shard_map/ppermute | solution.py:51
  69.1 9.9 %collective-permute-start.26 = (bf16[512,256]{1,0:T(8,128)(2,1)S(1)}, bf16[512,256]{1,0:T(8,128)(2,1)S(1)}, u32[]{:S(2)}, u32[]{:S(2)}) collective-permute-start(bf16[512,256]{1,0:T(8,128)(2,1)S(1)} %get-tuple-element.40), channel_id=1, source_target_pairs={{0,159},{1,128},{2,129},{3,130},{4,131},{5,132},{6,133},{7,134},{8... | collective-permute-start | bytes 786440 | tf_op jit(solution)/shard_map/ppermute | solution.py:42
  69.3 14.5 %collective-permute-start.24 = (bf16[512,256]{1,0:T(8,128)(2,1)S(1)}, bf16[512,256]{1,0:T(8,128)(2,1)S(1)}, u32[]{:S(2)}, u32[]{:S(2)}) collective-permute-start(bf16[512,256]{1,0:T(8,128)(2,1)S(1)} %get-tuple-element.40), channel_id=1, source_target_pairs={{0,129},{1,130},{2,131},{3,132},{4,133},{5,134},{6,135},{7,136},{8... | collective-permute-start | bytes 786440 | tf_op jit(solution)/shard_map/ppermute | solution.py:42
  71.0 25.5 %collective-permute-start.16 = (bf16[1536,384]{1,0:T(8,128)(2,1)S(1)}, bf16[1536,384]{1,0:T(8,128)(2,1)S(1)}, u32[]{:S(2)}, u32[]{:S(2)}) collective-permute-start(bf16[1536,384]{1,0:T(8,128)(2,1)S(1)} %out_half.1.w_own), channel_id=1, source_target_pairs={{0,128},{128,0},{1,129},{129,1},{2,130},{130,2},{3,131},{131,3},{4... | collective-permute-start | bytes 3538952 | tf_op jit(solution)/shard_map/ppermute | solution.py:51
  73.1 11.9 %collective-permute-start.25 = (bf16[512,256]{1,0:T(8,128)(2,1)S(1)}, bf16[512,256]{1,0:T(8,128)(2,1)S(1)}, u32[]{:S(2)}, u32[]{:S(2)}) collective-permute-start(bf16[512,256]{1,0:T(8,128)(2,1)S(1)} %get-tuple-element.44.refs_0_), channel_id=1, source_target_pairs={{0,31},{1,0},{2,1},{3,2},{4,3},{5,4},{6,5},{7,6},{8,7},{9,8},{10,9... | collective-permute-start | bytes 786440 | tf_op jit(solution)/shard_map/ppermute | solution.py:42
  76.8 10.5 %collective-permute-start.23 = (bf16[512,256]{1,0:T(8,128)(2,1)S(1)}, bf16[512,256]{1,0:T(8,128)(2,1)S(1)}, u32[]{:S(2)}, u32[]{:S(2)}) collective-permute-start(bf16[512,256]{1,0:T(8,128)(2,1)S(1)} %get-tuple-element.44.refs_0_), channel_id=1, source_target_pairs={{0,1},{1,2},{2,3},{3,4},{4,5},{5,6},{6,7},{7,8},{8,9},{9,10},{10,1... | collective-permute-start | bytes 786440 | tf_op jit(solution)/shard_map/ppermute | solution.py:42
  79.0 12.7 %collective-permute-start.31 = (bf16[512,256]{1,0:T(8,128)(2,1)S(1)}, bf16[512,256]{1,0:T(8,128)(2,1)S(1)}, u32[]{:S(2)}, u32[]{:S(2)}) collective-permute-start(bf16[512,256]{1,0:T(8,128)(2,1)S(1)} %pack.1), channel_id=1, source_target_pairs={{0,31},{1,0},{2,1},{3,2},{4,3},{5,4},{6,5},{7,6},{8,7},{9,8},{10,9... | collective-permute-start | bytes 786440 | tf_op jit(solution)/shard_map/ppermute | solution.py:42
  83.9 9.8 %collective-permute-start.30 = (bf16[512,256]{1,0:T(8,128)(2,1)S(1)}, bf16[512,256]{1,0:T(8,128)(2,1)S(1)}, u32[]{:S(2)}, u32[]{:S(2)}) collective-permute-start(bf16[512,256]{1,0:T(8,128)(2,1)S(1)} %pack.1), channel_id=1, source_target_pairs={{0,1},{1,2},{2,3},{3,4},{4,5},{5,6},{6,7},{7,8},{8,9},{9,10},{10,1... | collective-permute-start | bytes 786440 | tf_op jit(solution)/shard_map/ppermute | solution.py:42
  90.6 13.4 %collective-permute-start.28 = (bf16[512,256]{1,0:T(8,128)(2,1)S(1)}, bf16[512,256]{1,0:T(8,128)(2,1)S(1)}, u32[]{:S(2)}, u32[]{:S(2)}) collective-permute-start(bf16[512,256]{1,0:T(8,128)(2,1)S(1)} %attend_0.1.refs_0_), channel_id=1, source_target_pairs={{0,96},{32,0},{64,32},{96,64},{1,97},{33,1},{65,33},{97,65},{2,98}... | collective-permute-start | bytes 786440 | tf_op jit(solution)/shard_map/ppermute | solution.py:47
  91.7 13.1 %collective-permute-start.27 = (bf16[512,256]{1,0:T(8,128)(2,1)S(1)}, bf16[512,256]{1,0:T(8,128)(2,1)S(1)}, u32[]{:S(2)}, u32[]{:S(2)}) collective-permute-start(bf16[512,256]{1,0:T(8,128)(2,1)S(1)} %attend_0.1.refs_0_), channel_id=1, source_target_pairs={{0,32},{32,64},{64,96},{96,0},{1,33},{33,65},{65,97},{97,1},{2,34}... | collective-permute-start | bytes 786440 | tf_op jit(solution)/shard_map/ppermute | solution.py:47
  94.5 11.4 %collective-permute-start.34 = (bf16[512,128]{1,0:T(8,128)(2,1)S(1)}, bf16[512,128]{1,0:T(8,128)(2,1)S(1)}, u32[]{:S(2)}, u32[]{:S(2)}) collective-permute-start(bf16[512,128]{1,0:T(8,128)(2,1)S(1)} %attend_1.1.refs_0_), channel_id=1, source_target_pairs={{0,64},{32,96},{64,0},{96,32},{1,65},{33,97},{65,1},{97,33},{2,66}... | collective-permute-start | bytes 393224 | tf_op jit(solution)/shard_map/ppermute | solution.py:47
  96.5 12.1 %collective-permute-start.33 = (bf16[512,128]{1,0:T(8,128)(2,1)S(1)}, bf16[512,128]{1,0:T(8,128)(2,1)S(1)}, u32[]{:S(2)}, u32[]{:S(2)}) collective-permute-start(bf16[512,128]{1,0:T(8,128)(2,1)S(1)} %attend_1.1.refs_0_), channel_id=1, source_target_pairs={{0,96},{32,0},{64,32},{96,64},{1,97},{33,1},{65,33},{97,65},{2,98}... | collective-permute-start | bytes 393224 | tf_op jit(solution)/shard_map/ppermute | solution.py:47
  97.5 11.5 %collective-permute-start.32 = (bf16[512,128]{1,0:T(8,128)(2,1)S(1)}, bf16[512,128]{1,0:T(8,128)(2,1)S(1)}, u32[]{:S(2)}, u32[]{:S(2)}) collective-permute-start(bf16[512,128]{1,0:T(8,128)(2,1)S(1)} %attend_1.1.refs_0_), channel_id=1, source_target_pairs={{0,32},{32,64},{64,96},{96,0},{1,33},{33,65},{65,97},{97,1},{2,34}... | collective-permute-start | bytes 393224 | tf_op jit(solution)/shard_map/ppermute | solution.py:47
  (16 other events, 154.7 us)

commit v3 on v2

--- a/solution.py
+++ b/solution.py
@@ -80,7 +80,8 @@
     p5, p4 = moved(p3, (1, 0), (0, 1)), moved(p2, (-1, 0), (0, -1))
     pieces = (tokens, below, above, far_top, far_bottom)
     others = [swapped(x) for x in pieces]
-    *others[3:], p5, p4 = lax.optimization_barrier((*others[3:], p5, p4))
+    others[3], p5 = lax.optimization_barrier((others[3], p5))
+    others[4], p4 = lax.optimization_barrier((others[4], p4))
     p7, p6 = moved(p5, (1, 0), (0, 1)), moved(p4, (-1, 0), (0, -1))
     return pieces, others, (s, p1, p2, p3, p4, p5, p6, p7)
 
@@ -349,12 +350,6 @@
         (norm_gains, w_q, w_q_other, *tokens),
         [pltpu.VMEM((NX * feats, width), BF)], 2**35, 6 * 2**20, 20, "query",
     )
-    late, _ = lax.optimization_barrier((same[1], query))
-    packed = call(
-        pack_kernel, jax.ShapeDtypeStruct((rows, 2 * late.shape[1]), BF),
-        (late, others_kv[1]), [], 0, 2**19, 8, "pack",
-    )
-    sides = [(a0, b0, a1, b1), tuple(frames_on(packed, step, False) for step in (1, -1))]
     scale = HD ** (-0.5) * math.log2(math.e)
     acc = call(
         functools.partial(own_kernel, scale),
@@ -362,6 +357,12 @@
         (neighbours, query, same[0], others_kv[0], same[1], others_kv[1]),
         [], 2**35, 6 * 2**20, 20, "own_frame",
     )
+    late, _ = lax.optimization_barrier((same[1], acc))
+    packed = call(
+        pack_kernel, jax.ShapeDtypeStruct((rows, 2 * late.shape[1]), BF),
+        (late, others_kv[1]), [], 0, 2**19, 8, "pack",
+    )
+    sides = [(a0, b0, a1, b1), tuple(frames_on(packed, step, False) for step in (1, -1))]
     first = depth * 3 // 2
     w_out = half_of(buffers, first, mine.shape[0] - first, "out_half")
     w_outs = (w_out, swapped(w_out))

time: 111 us -> 111 us (level)
  waiting for transfers between devices: 44.7 us -> 40.8 us
  starting transfers between devices: 51 us -> 54.8 us
    ppermute x10, waiting for transfers between devices: 28 us -> 25.5 us  [moved(): return lax.ppermute(x, ('dp', 'head'), pairs)]
    ppermute x10, starting transfers between devices: 19.5 us -> 21.4 us  [moved(): return lax.ppermute(x, ('dp', 'head'), pairs)]
    ppermute x9, waiting for transfers between devices: 1.92 us -> 0.02 us  [swapped(): return lax.ppermute(x, 'dp', [(0, 1), (1, 0)])]
    ppermute x9, starting transfers between devices: 8.16 us -> 10 us  [swapped(): return lax.ppermute(x, 'dp', [(0, 1), (1, 0)])]
  transfers between devices with their start and end apart: 35 -> 35, of which waited for: 18 -> 16; matrix products, arithmetic and copies ran while one was open for 0% -> 0% of each run, Pallas kernels for 10% -> 10%
where the time goes in v3:
time: 111 us
  starting transfers between devices  54.8 us (49%)
  waiting for transfers between devices  40.8 us (37%)
  Pallas kernels  12.9 us (12%)
  local copies, waits for them, and re-layouts  1.84 us (2%)
    ppermute x10, waiting for transfers between devices, moved(): return lax.ppermute(x, ('dp', 'head'), pairs)  25.5 us
    ppermute x10, starting transfers between devices, moved(): return lax.ppermute(x, ('dp', 'head'), pairs)  21.4 us
    ppermute x10, starting transfers between devices, along(): return lax.ppermute(x, axis, [(i, (i + step) % n) for i in range(n)])  13.1 us
    pallas_call x13, Pallas kernels, call(): pl.pallas_call(kernel, out_shape=out_shape, in_specs=[VMEM] * n, out_spec...  12.9 us
    ppermute x10, waiting for transfers between devices, along(): return lax.ppermute(x, axis, [(i, (i + step) % n) for i in range(n)])  10.3 us
    ppermute x6, starting transfers between devices, frames_on(): return lax.ppermute(x, ('dp', 'head'), pairs)  10.3 us
    ppermute x9, starting transfers between devices, swapped(): return lax.ppermute(x, 'dp', [(0, 1), (1, 0)])  10 us
    ppermute x6, waiting for transfers between devices, frames_on(): return lax.ppermute(x, ('dp', 'head'), pairs)  4.9 us
  transfers between devices with their start and end apart: 35, of which 16 were waited for; matrix products, arithmetic and copies ran while one was open for 0% of the time, Pallas kernels for 10%

profile of v3, /device:TPU:1, one launch (start us, length us, event | category | flops | bytes accessed | tf_op | source)
XLA Modules:
  0.0 110.6 jit_solution(4300629790273902243)
XLA Ops:
  0.0 3.3 %collective-permute-start.1 = (bf16[512,768]{1,0:T(8,128)(2,1)}, bf16[512,768]{1,0:T(8,128)(2,1)S(1)}, u32[]{:S(2)}, u32[]{:S(2)}) collective-permute-start(bf16[512,768]{1,0:T(8,128)(2,1)} %refs_0_.3), channel_id=1, source_target_pairs={{0,96},{32,0},{64,32},{96,64},{1,97},{33,1},{65,33},{97,65},{2,98}... | collective-permute-start | bytes 2359304 | tf_op jit(solution)/shard_map/ppermute | solution.py:47
  5.2 7.0 %collective-permute-start.4 = (bf16[192,384]{1,0:T(8,128)(2,1)S(1)}, bf16[192,384]{1,0:T(8,128)(2,1)S(1)}, u32[]{:S(2)}, u32[]{:S(2)}) collective-permute-start(bf16[192,384]{1,0:T(8,128)(2,1)S(1)} %prepare.1), channel_id=1, source_target_pairs={{0,2},{1,3},{2,0},{3,1},{4,6},{5,7},{6,4},{7,5},{8,10},{9,11},{10,... | collective-permute-start | bytes 442376 | tf_op jit(solution)/shard_map/ppermute | solution.py:33
  12.2 2.4 %collective-permute-start.2 = (bf16[192,384]{1,0:T(8,128)(2,1)S(1)}, bf16[192,384]{1,0:T(8,128)(2,1)S(1)}, u32[]{:S(2)}, u32[]{:S(2)}) collective-permute-start(bf16[192,384]{1,0:T(8,128)(2,1)S(1)} %prepare.1), channel_id=1, source_target_pairs={{0,1},{1,2},{2,3},{3,0},{4,5},{5,6},{6,7},{7,4},{8,9},{9,10},{10,1... | collective-permute-start | bytes 442376 | tf_op jit(solution)/shard_map/ppermute | solution.py:33
  14.8 5.4 %collective-permute-done.3 = bf16[192,384]{1,0:T(8,128)(2,1)S(1)} collective-permute-done((bf16[192,384]{1,0:T(8,128)(2,1)S(1)}, bf16[192,384]{1,0:T(8,128)(2,1)S(1)}, u32[]{:S(2)}, u32[]{:S(2)}) %collective-permute-start.3) | collective-permute-done | bytes 147488 | tf_op jit(solution)/shard_map/ppermute | solution.py:33
  20.3 2.5 %collective-permute-start.5 = (bf16[768,384]{1,0:T(8,128)(2,1)S(1)}, bf16[768,384]{1,0:T(8,128)(2,1)S(1)}, u32[]{:S(2)}, u32[]{:S(2)}) collective-permute-start(bf16[768,384]{1,0:T(8,128)(2,1)S(1)} %pad_maximum_fusion.refs_0_.refs_5_), channel_id=1, source_target_pairs={{0,4},{1,5},{2,6},{3,7},{4,8},{5,9},{6,10},{7,11},{8,12},{9,13},{1... | collective-permute-start | bytes 1769480 | tf_op jit(solution)/shard_map/ppermute | solution.py:33
  22.9 6.7 %collective-permute-done.5.refs_1_.refs_6_ = bf16[768,384]{1,0:T(8,128)(2,1)S(1)} collective-permute-done((bf16[768,384]{1,0:T(8,128)(2,1)S(1)}, bf16[768,384]{1,0:T(8,128)(2,1)S(1)}, u32[]{:S(2)}, u32[]{:S(2)}) %collective-permute-start.5) | collective-permute-done | bytes 589856 | tf_op jit(solution)/shard_map/ppermute | solution.py:33
  29.6 2.7 %collective-permute-start.6 = (bf16[768,384]{1,0:T(8,128)(2,1)S(1)}, bf16[768,384]{1,0:T(8,128)(2,1)S(1)}, u32[]{:S(2)}, u32[]{:S(2)}) collective-permute-start(bf16[768,384]{1,0:T(8,128)(2,1)S(1)} %pad_maximum_fusion.refs_0_.refs_5_), channel_id=1, source_target_pairs={{0,28},{1,29},{2,30},{3,31},{4,0},{5,1},{6,2},{7,3},{8,4},{9,5},{1... | collective-permute-start | bytes 1769480 | tf_op jit(solution)/shard_map/ppermute | solution.py:33
  32.3 2.7 %collective-permute-start.8 = (bf16[256,768]{1,0:T(8,128)(2,1)S(1)}, bf16[256,768]{1,0:T(8,128)(2,1)S(1)}, u32[]{:S(2)}, u32[]{:S(2)}) collective-permute-start(bf16[256,768]{1,0:T(8,128)(2,1)S(1)} %get-tuple-element.31), channel_id=1, source_target_pairs={{0,96},{32,0},{64,32},{96,64},{1,97},{33,1},{65,33},{97,65},{2,98}... | collective-permute-start | bytes 1179656 | tf_op jit(solution)/shard_map/ppermute | solution.py:47
  35.0 4.1 %collective-permute-done.6.refs_2_.refs_7_ = bf16[768,384]{1,0:T(8,128)(2,1)S(1)} collective-permute-done((bf16[768,384]{1,0:T(8,128)(2,1)S(1)}, bf16[768,384]{1,0:T(8,128)(2,1)S(1)}, u32[]{:S(2)}, u32[]{:S(2)}) %collective-permute-start.6) | collective-permute-done | bytes 589856 | tf_op jit(solution)/shard_map/ppermute | solution.py:33
  39.2 3.4 %collective-permute-start.10 = (bf16[768,384]{1,0:T(8,128)(2,1)S(1)}, bf16[768,384]{1,0:T(8,128)(2,1)S(1)}, u32[]{:S(2)}, u32[]{:S(2)}) collective-permute-start(bf16[768,384]{1,0:T(8,128)(2,1)S(1)} %collective-permute-done.6.refs_2_.refs_7_), channel_id=1, source_target_pairs={{0,28},{1,29},{2,30},{3,31},{4,0},{5,1},{6,2},{7,3},{8,4},{9,5},{1... | collective-permute-start | bytes 1769480 | tf_op jit(solution)/shard_map/ppermute | solution.py:33
  49.4 3.4 %collective-permute-start.14 = (bf16[768,384]{1,0:T(8,128)(2,1)S(1)}, bf16[768,384]{1,0:T(8,128)(2,1)S(1)}, u32[]{:S(2)}, u32[]{:S(2)}) collective-permute-start(bf16[768,384]{1,0:T(8,128)(2,1)S(1)} %collective-permute-done.10.refs_4_.refs_9_), channel_id=1, source_target_pairs={{0,28},{1,29},{2,30},{3,31},{4,0},{5,1},{6,2},{7,3},{8,4},{9,5},{1... | collective-permute-start | bytes 1769480 | tf_op jit(solution)/shard_map/ppermute | solution.py:33
  52.8 2.4 %collective-permute-start.18 = (bf16[512,768]{1,0:T(8,128)(2,1)S(1)}, bf16[512,768]{1,0:T(8,128)(2,1)S(1)}, u32[]{:S(2)}, u32[]{:S(2)}) collective-permute-start(bf16[512,768]{1,0:T(8,128)(2,1)S(1)} %copy-done), channel_id=1, source_target_pairs={{0,128},{128,0},{1,129},{129,1},{2,130},{130,2},{3,131},{131,3},{4... | collective-permute-start | bytes 2359304 | tf_op jit(solution)/shard_map/ppermute | solution.py:51
  55.7 3.9 %collective-permute-done.14.refs_6_.refs_11_ = bf16[768,384]{1,0:T(8,128)(2,1)S(1)} collective-permute-done((bf16[768,384]{1,0:T(8,128)(2,1)S(1)}, bf16[768,384]{1,0:T(8,128)(2,1)S(1)}, u32[]{:S(2)}, u32[]{:S(2)}) %collective-permute-start.14) | collective-permute-done | bytes 589856 | tf_op jit(solution)/shard_map/ppermute | solution.py:33
  59.6 3.4 %collective-permute-done.15.refs_7_.refs_12_ = bf16[768,384]{1,0:T(8,128)(2,1)S(1)} collective-permute-done((bf16[768,384]{1,0:T(8,128)(2,1)S(1)}, bf16[768,384]{1,0:T(8,128)(2,1)S(1)}, u32[]{:S(2)}, u32[]{:S(2)}) %collective-permute-start.15) | collective-permute-done | bytes 589856 | tf_op jit(solution)/shard_map/ppermute | solution.py:33
  63.2 3.0 %collective-permute-start.17 = (bf16[1536,384]{1,0:T(8,128)(2,1)S(1)}, bf16[1536,384]{1,0:T(8,128)(2,1)S(1)}, u32[]{:S(2)}, u32[]{:S(2)}) collective-permute-start(bf16[1536,384]{1,0:T(8,128)(2,1)S(1)} %query_half.1.w_own), channel_id=1, source_target_pairs={{0,128},{128,0},{1,129},{129,1},{2,130},{130,2},{3,131},{131,3},{4... | collective-permute-start | bytes 3538952 | tf_op jit(solution)/shard_map/ppermute | solution.py:51
  66.2 2.2 %project_cross.1 = (bf16[512,256]{1,0:T(8,128)(2,1)S(1)}, bf16[512,128]{1,0:T(8,128)(2,1)S(1)}, bf16[3072,384]{1,0:T(8,128)(2,1)S(1)}) custom-call(f32[2,128]{1,0:T(2,128)S(1)} %copy-done.1, bf16[512,768]{1,0:T(8,128)(2,1)S(1)} %collective-permute-done.18.refs_0_, bf16[512,768]{1,0:T(8,128)(2,1)S(1)} %collective-permute-done.19.refs_1_, ...), custom_call_target="tpu_custom_call" | custom-call | flops 1207959552 | bytes 6291456 | tf_op jit(solution)/shard_map/project_cross/pallas_call | solution.py:119
  73.1 3.7 %collective-permute-start.25 = (bf16[512,256]{1,0:T(8,128)(2,1)S(1)}, bf16[512,256]{1,0:T(8,128)(2,1)S(1)}, u32[]{:S(2)}, u32[]{:S(2)}) collective-permute-start(bf16[512,256]{1,0:T(8,128)(2,1)S(1)} %get-tuple-element.44.refs_0_), channel_id=1, source_target_pairs={{0,31},{1,0},{2,1},{3,2},{4,3},{5,4},{6,5},{7,6},{8,7},{9,8},{10,9... | collective-permute-start | bytes 786440 | tf_op jit(solution)/shard_map/ppermute | solution.py:42
  76.8 2.1 %query.1.q_ref = bf16[512,384]{1,0:T(8,128)(2,1)S(1)} custom-call(f32[2,128]{1,0:T(2,128)S(1)} %copy-done.1, bf16[1536,384]{1,0:T(8,128)(2,1)S(1)} %query_half.1.w_own, bf16[1536,384]{1,0:T(8,128)(2,1)S(1)} %collective-permute-done.17.w_other, bf16[512,768]{1,0:T(8,128)(2,1)S(1)} %copy-done, bf16[512,768]{1,0:T(8,128)(2,1)S(1)} %collective-permute-done.below.refs_1_, ...), custom_call_target="tpu_custom_call" | custom-call | flops 34359738368 | bytes 6291456 | tf_op jit(solution)/shard_map/query/pallas_call | solution.py:119
  80.1 4.9 %collective-permute-start.31 = (bf16[512,256]{1,0:T(8,128)(2,1)S(1)}, bf16[512,256]{1,0:T(8,128)(2,1)S(1)}, u32[]{:S(2)}, u32[]{:S(2)}) collective-permute-start(bf16[512,256]{1,0:T(8,128)(2,1)S(1)} %pack.1), channel_id=1, source_target_pairs={{0,31},{1,0},{2,1},{3,2},{4,3},{5,4},{6,5},{7,6},{8,7},{9,8},{10,9... | collective-permute-start | bytes 786440 | tf_op jit(solution)/shard_map/ppermute | solution.py:42
  85.0 2.2 %collective-permute-done.23.refs_0_ = bf16[512,256]{1,0:T(8,128)(2,1)S(1)} collective-permute-done((bf16[512,256]{1,0:T(8,128)(2,1)S(1)}, bf16[512,256]{1,0:T(8,128)(2,1)S(1)}, u32[]{:S(2)}, u32[]{:S(2)}) %collective-permute-start.23) | collective-permute-done | bytes 262176 | tf_op jit(solution)/shard_map/ppermute | solution.py:42
  88.6 2.0 %collective-permute-start.29 = (bf16[512,256]{1,0:T(8,128)(2,1)S(1)}, bf16[512,256]{1,0:T(8,128)(2,1)S(1)}, u32[]{:S(2)}, u32[]{:S(2)}) collective-permute-start(bf16[512,256]{1,0:T(8,128)(2,1)S(1)} %attend_0.1.refs_0_), channel_id=1, source_target_pairs={{0,64},{32,96},{64,0},{96,32},{1,65},{33,97},{65,1},{97,33},{2,66}... | collective-permute-start | bytes 786440 | tf_op jit(solution)/shard_map/ppermute | solution.py:47
  92.2 2.7 %collective-permute-done.30.refs_0_ = bf16[512,256]{1,0:T(8,128)(2,1)S(1)} collective-permute-done((bf16[512,256]{1,0:T(8,128)(2,1)S(1)}, bf16[512,256]{1,0:T(8,128)(2,1)S(1)}, u32[]{:S(2)}, u32[]{:S(2)}) %collective-permute-start.30) | collective-permute-done | bytes 262176 | tf_op jit(solution)/shard_map/ppermute | solution.py:42
  99.3 4.7 %collective-permute-done.28.refs_2_ = bf16[512,256]{1,0:T(8,128)(2,1)S(1)} collective-permute-done((bf16[512,256]{1,0:T(8,128)(2,1)S(1)}, bf16[512,256]{1,0:T(8,128)(2,1)S(1)}, u32[]{:S(2)}, u32[]{:S(2)}) %collective-permute-start.28) | collective-permute-done | bytes 262176 | tf_op jit(solution)/shard_map/ppermute | solution.py:47
  106.0 2.6 %collective-permute-done.33.refs_2_ = bf16[512,128]{1,0:T(8,128)(2,1)S(1)} collective-permute-done((bf16[512,128]{1,0:T(8,128)(2,1)S(1)}, bf16[512,128]{1,0:T(8,128)(2,1)S(1)}, u32[]{:S(2)}, u32[]{:S(2)}) %collective-permute-start.33) | collective-permute-done | bytes 131104 | tf_op jit(solution)/shard_map/ppermute | solution.py:47
  (70 shorter events, 26.9 us)
Async XLA Ops:
  0.0 22.8 %collective-permute-start.1 = (bf16[512,768]{1,0:T(8,128)(2,1)}, bf16[512,768]{1,0:T(8,128)(2,1)S(1)}, u32[]{:S(2)}, u32[]{:S(2)}) collective-permute-start(bf16[512,768]{1,0:T(8,128)(2,1)} %refs_0_.3), channel_id=1, source_target_pairs={{0,96},{32,0},{64,32},{96,64},{1,97},{33,1},{65,33},{97,65},{2,98}... | collective-permute-start | bytes 2359304 | tf_op jit(solution)/shard_map/ppermute | solution.py:47
  3.3 19.5 %collective-permute-start = (bf16[512,768]{1,0:T(8,128)(2,1)}, bf16[512,768]{1,0:T(8,128)(2,1)S(1)}, u32[]{:S(2)}, u32[]{:S(2)}) collective-permute-start(bf16[512,768]{1,0:T(8,128)(2,1)} %refs_0_.3), channel_id=1, source_target_pairs={{0,32},{32,64},{64,96},{96,0},{1,33},{33,65},{65,97},{97,1},{2,34}... | collective-permute-start | bytes 2359304 | tf_op jit(solution)/shard_map/ppermute | solution.py:47
  32.3 10.2 %collective-permute-start.7 = (bf16[768,384]{1,0:T(8,128)(2,1)S(1)}, bf16[768,384]{1,0:T(8,128)(2,1)S(1)}, u32[]{:S(2)}, u32[]{:S(2)}) collective-permute-start(bf16[768,384]{1,0:T(8,128)(2,1)S(1)} %collective-permute-done.5.refs_1_.refs_6_), channel_id=1, source_target_pairs={{0,4},{1,5},{2,6},{3,7},{4,8},{5,9},{6,10},{7,11},{8,12},{9,13},{1... | collective-permute-start | bytes 1769480 | tf_op jit(solution)/shard_map/ppermute | solution.py:33
  32.3 10.5 %collective-permute-start.8 = (bf16[256,768]{1,0:T(8,128)(2,1)S(1)}, bf16[256,768]{1,0:T(8,128)(2,1)S(1)}, u32[]{:S(2)}, u32[]{:S(2)}) collective-permute-start(bf16[256,768]{1,0:T(8,128)(2,1)S(1)} %get-tuple-element.31), channel_id=1, source_target_pairs={{0,96},{32,0},{64,32},{96,64},{1,97},{33,1},{65,33},{97,65},{2,98}... | collective-permute-start | bytes 1179656 | tf_op jit(solution)/shard_map/ppermute | solution.py:47
  35.0 10.9 %collective-permute-start.11 = (bf16[256,768]{1,0:T(8,128)(2,1)S(1)}, bf16[256,768]{1,0:T(8,128)(2,1)S(1)}, u32[]{:S(2)}, u32[]{:S(2)}) collective-permute-start(bf16[256,768]{1,0:T(8,128)(2,1)S(1)} %get-tuple-element.33), channel_id=1, source_target_pairs={{0,32},{32,64},{64,96},{96,0},{1,33},{33,65},{65,97},{97,1},{2,34}... | collective-permute-start | bytes 1179656 | tf_op jit(solution)/shard_map/ppermute | solution.py:47
  39.2 10.2 %collective-permute-start.10 = (bf16[768,384]{1,0:T(8,128)(2,1)S(1)}, bf16[768,384]{1,0:T(8,128)(2,1)S(1)}, u32[]{:S(2)}, u32[]{:S(2)}) collective-permute-start(bf16[768,384]{1,0:T(8,128)(2,1)S(1)} %collective-permute-done.6.refs_2_.refs_7_), channel_id=1, source_target_pairs={{0,28},{1,29},{2,30},{3,31},{4,0},{5,1},{6,2},{7,3},{8,4},{9,5},{1... | collective-permute-start | bytes 1769480 | tf_op jit(solution)/shard_map/ppermute | solution.py:33
  42.6 10.2 %collective-permute-start.13 = (bf16[768,384]{1,0:T(8,128)(2,1)S(1)}, bf16[768,384]{1,0:T(8,128)(2,1)S(1)}, u32[]{:S(2)}, u32[]{:S(2)}) collective-permute-start(bf16[768,384]{1,0:T(8,128)(2,1)S(1)} %collective-permute-done.7.refs_3_.refs_8_), channel_id=1, source_target_pairs={{0,4},{1,5},{2,6},{3,7},{4,8},{5,9},{6,10},{7,11},{8,12},{9,13},{1... | collective-permute-start | bytes 1769480 | tf_op jit(solution)/shard_map/ppermute | solution.py:33
  49.4 10.2 %collective-permute-start.14 = (bf16[768,384]{1,0:T(8,128)(2,1)S(1)}, bf16[768,384]{1,0:T(8,128)(2,1)S(1)}, u32[]{:S(2)}, u32[]{:S(2)}) collective-permute-start(bf16[768,384]{1,0:T(8,128)(2,1)S(1)} %collective-permute-done.10.refs_4_.refs_9_), channel_id=1, source_target_pairs={{0,28},{1,29},{2,30},{3,31},{4,0},{5,1},{6,2},{7,3},{8,4},{9,5},{1... | collective-permute-start | bytes 1769480 | tf_op jit(solution)/shard_map/ppermute | solution.py:33
  52.8 10.2 %collective-permute-start.15 = (bf16[768,384]{1,0:T(8,128)(2,1)S(1)}, bf16[768,384]{1,0:T(8,128)(2,1)S(1)}, u32[]{:S(2)}, u32[]{:S(2)}) collective-permute-start(bf16[768,384]{1,0:T(8,128)(2,1)S(1)} %collective-permute-done.13.refs_5_.refs_10_), channel_id=1, source_target_pairs={{0,4},{1,5},{2,6},{3,7},{4,8},{5,9},{6,10},{7,11},{8,12},{9,13},{1... | collective-permute-start | bytes 1769480 | tf_op jit(solution)/shard_map/ppermute | solution.py:33
  52.8 13.4 %collective-permute-start.18 = (bf16[512,768]{1,0:T(8,128)(2,1)S(1)}, bf16[512,768]{1,0:T(8,128)(2,1)S(1)}, u32[]{:S(2)}, u32[]{:S(2)}) collective-permute-start(bf16[512,768]{1,0:T(8,128)(2,1)S(1)} %copy-done), channel_id=1, source_target_pairs={{0,128},{128,0},{1,129},{129,1},{2,130},{130,2},{3,131},{131,3},{4... | collective-permute-start | bytes 2359304 | tf_op jit(solution)/shard_map/ppermute | solution.py:51
  55.2 11.0 %collective-permute-start.19 = (bf16[512,768]{1,0:T(8,128)(2,1)S(1)}, bf16[512,768]{1,0:T(8,128)(2,1)S(1)}, u32[]{:S(2)}, u32[]{:S(2)}) collective-permute-start(bf16[512,768]{1,0:T(8,128)(2,1)S(1)} %collective-permute-done.below.refs_1_), channel_id=1, source_target_pairs={{0,128},{128,0},{1,129},{129,1},{2,130},{130,2},{3,131},{131,3},{4... | collective-permute-start | bytes 2359304 | tf_op jit(solution)/shard_map/ppermute | solution.py:51
  55.3 10.9 %collective-permute-start.20 = (bf16[512,768]{1,0:T(8,128)(2,1)S(1)}, bf16[512,768]{1,0:T(8,128)(2,1)S(1)}, u32[]{:S(2)}, u32[]{:S(2)}) collective-permute-start(bf16[512,768]{1,0:T(8,128)(2,1)S(1)} %collective-permute-done.1.above.refs_2_), channel_id=1, source_target_pairs={{0,128},{128,0},{1,129},{129,1},{2,130},{130,2},{3,131},{131,3},{4... | collective-permute-start | bytes 2359304 | tf_op jit(solution)/shard_map/ppermute | solution.py:51
  63.2 13.6 %collective-permute-start.17 = (bf16[1536,384]{1,0:T(8,128)(2,1)S(1)}, bf16[1536,384]{1,0:T(8,128)(2,1)S(1)}, u32[]{:S(2)}, u32[]{:S(2)}) collective-permute-start(bf16[1536,384]{1,0:T(8,128)(2,1)S(1)} %query_half.1.w_own), channel_id=1, source_target_pairs={{0,128},{128,0},{1,129},{129,1},{2,130},{130,2},{3,131},{131,3},{4... | collective-permute-start | bytes 3538952 | tf_op jit(solution)/shard_map/ppermute | solution.py:51
  69.1 11.0 %collective-permute-start.26 = (bf16[512,256]{1,0:T(8,128)(2,1)S(1)}, bf16[512,256]{1,0:T(8,128)(2,1)S(1)}, u32[]{:S(2)}, u32[]{:S(2)}) collective-permute-start(bf16[512,256]{1,0:T(8,128)(2,1)S(1)} %get-tuple-element.40), channel_id=1, source_target_pairs={{0,159},{1,128},{2,129},{3,130},{4,131},{5,132},{6,133},{7,134},{8... | collective-permute-start | bytes 786440 | tf_op jit(solution)/shard_map/ppermute | solution.py:42
  69.3 15.7 %collective-permute-start.24 = (bf16[512,256]{1,0:T(8,128)(2,1)S(1)}, bf16[512,256]{1,0:T(8,128)(2,1)S(1)}, u32[]{:S(2)}, u32[]{:S(2)}) collective-permute-start(bf16[512,256]{1,0:T(8,128)(2,1)S(1)} %get-tuple-element.40), channel_id=1, source_target_pairs={{0,129},{1,130},{2,131},{3,132},{4,133},{5,134},{6,135},{7,136},{8... | collective-permute-start | bytes 786440 | tf_op jit(solution)/shard_map/ppermute | solution.py:42
  71.0 26.7 %collective-permute-start.16 = (bf16[1536,384]{1,0:T(8,128)(2,1)S(1)}, bf16[1536,384]{1,0:T(8,128)(2,1)S(1)}, u32[]{:S(2)}, u32[]{:S(2)}) collective-permute-start(bf16[1536,384]{1,0:T(8,128)(2,1)S(1)} %out_half.1.w_own), channel_id=1, source_target_pairs={{0,128},{128,0},{1,129},{129,1},{2,130},{130,2},{3,131},{131,3},{4... | collective-permute-start | bytes 3538952 | tf_op jit(solution)/shard_map/ppermute | solution.py:51
  73.1 11.9 %collective-permute-start.25 = (bf16[512,256]{1,0:T(8,128)(2,1)S(1)}, bf16[512,256]{1,0:T(8,128)(2,1)S(1)}, u32[]{:S(2)}, u32[]{:S(2)}) collective-permute-start(bf16[512,256]{1,0:T(8,128)(2,1)S(1)} %get-tuple-element.44.refs_0_), channel_id=1, source_target_pairs={{0,31},{1,0},{2,1},{3,2},{4,3},{5,4},{6,5},{7,6},{8,7},{9,8},{10,9... | collective-permute-start | bytes 786440 | tf_op jit(solution)/shard_map/ppermute | solution.py:42
  76.8 10.5 %collective-permute-start.23 = (bf16[512,256]{1,0:T(8,128)(2,1)S(1)}, bf16[512,256]{1,0:T(8,128)(2,1)S(1)}, u32[]{:S(2)}, u32[]{:S(2)}) collective-permute-start(bf16[512,256]{1,0:T(8,128)(2,1)S(1)} %get-tuple-element.44.refs_0_), channel_id=1, source_target_pairs={{0,1},{1,2},{2,3},{3,4},{4,5},{5,6},{6,7},{7,8},{8,9},{9,10},{10,1... | collective-permute-start | bytes 786440 | tf_op jit(solution)/shard_map/ppermute | solution.py:42
  80.1 11.6 %collective-permute-start.31 = (bf16[512,256]{1,0:T(8,128)(2,1)S(1)}, bf16[512,256]{1,0:T(8,128)(2,1)S(1)}, u32[]{:S(2)}, u32[]{:S(2)}) collective-permute-start(bf16[512,256]{1,0:T(8,128)(2,1)S(1)} %pack.1), channel_id=1, source_target_pairs={{0,31},{1,0},{2,1},{3,2},{4,3},{5,4},{6,5},{7,6},{8,7},{9,8},{10,9... | collective-permute-start | bytes 786440 | tf_op jit(solution)/shard_map/ppermute | solution.py:42
  90.6 13.4 %collective-permute-start.28 = (bf16[512,256]{1,0:T(8,128)(2,1)S(1)}, bf16[512,256]{1,0:T(8,128)(2,1)S(1)}, u32[]{:S(2)}, u32[]{:S(2)}) collective-permute-start(bf16[512,256]{1,0:T(8,128)(2,1)S(1)} %attend_0.1.refs_0_), channel_id=1, source_target_pairs={{0,96},{32,0},{64,32},{96,64},{1,97},{33,1},{65,33},{97,65},{2,98}... | collective-permute-start | bytes 786440 | tf_op jit(solution)/shard_map/ppermute | solution.py:47
  91.7 13.0 %collective-permute-start.27 = (bf16[512,256]{1,0:T(8,128)(2,1)S(1)}, bf16[512,256]{1,0:T(8,128)(2,1)S(1)}, u32[]{:S(2)}, u32[]{:S(2)}) collective-permute-start(bf16[512,256]{1,0:T(8,128)(2,1)S(1)} %attend_0.1.refs_0_), channel_id=1, source_target_pairs={{0,32},{32,64},{64,96},{96,0},{1,33},{33,65},{65,97},{97,1},{2,34}... | collective-permute-start | bytes 786440 | tf_op jit(solution)/shard_map/ppermute | solution.py:47
  95.7 10.3 %collective-permute-start.34 = (bf16[512,128]{1,0:T(8,128)(2,1)S(1)}, bf16[512,128]{1,0:T(8,128)(2,1)S(1)}, u32[]{:S(2)}, u32[]{:S(2)}) collective-permute-start(bf16[512,128]{1,0:T(8,128)(2,1)S(1)} %attend_1.1.refs_0_), channel_id=1, source_target_pairs={{0,64},{32,96},{64,0},{96,32},{1,65},{33,97},{65,1},{97,33},{2,66}... | collective-permute-start | bytes 393224 | tf_op jit(solution)/shard_map/ppermute | solution.py:47
  97.6 11.0 %collective-permute-start.33 = (bf16[512,128]{1,0:T(8,128)(2,1)S(1)}, bf16[512,128]{1,0:T(8,128)(2,1)S(1)}, u32[]{:S(2)}, u32[]{:S(2)}) collective-permute-start(bf16[512,128]{1,0:T(8,128)(2,1)S(1)} %attend_1.1.refs_0_), channel_id=1, source_target_pairs={{0,96},{32,0},{64,32},{96,64},{1,97},{33,1},{65,33},{97,65},{2,98}... | collective-permute-start | bytes 393224 | tf_op jit(solution)/shard_map/ppermute | solution.py:47
  98.7 10.3 %collective-permute-start.32 = (bf16[512,128]{1,0:T(8,128)(2,1)S(1)}, bf16[512,128]{1,0:T(8,128)(2,1)S(1)}, u32[]{:S(2)}, u32[]{:S(2)}) collective-permute-start(bf16[512,128]{1,0:T(8,128)(2,1)S(1)} %attend_1.1.refs_0_), channel_id=1, source_target_pairs={{0,32},{32,64},{64,96},{96,0},{1,33},{33,65},{65,97},{97,1},{2,34}... | collective-permute-start | bytes 393224 | tf_op jit(solution)/shard_map/ppermute | solution.py:47
  (16 other events, 158.3 us)

commit v4 on v2

--- a/solution.py
+++ b/solution.py
@@ -80,7 +80,8 @@
     p5, p4 = moved(p3, (1, 0), (0, 1)), moved(p2, (-1, 0), (0, -1))
     pieces = (tokens, below, above, far_top, far_bottom)
     others = [swapped(x) for x in pieces]
-    *others[3:], p5, p4 = lax.optimization_barrier((*others[3:], p5, p4))
+    others[3], p5 = lax.optimization_barrier((others[3], p5))
+    others[4], p4 = lax.optimization_barrier((others[4], p4))
     p7, p6 = moved(p5, (1, 0), (0, 1)), moved(p4, (-1, 0), (0, -1))
     return pieces, others, (s, p1, p2, p3, p4, p5, p6, p7)
 
@@ -223,7 +224,7 @@
     rows, keys = q.shape[0], key.shape[0]
     score = lax.dot_general(q, key, (((1,), (1,)), ((), ())), preferred_element_type=F32)
     weight = jnp.exp2(score * scale).reshape(rows // TILE, TILE, keys)
-    weight = jnp.where(keep[:, None, :] > 0, weight, 0.0).reshape(rows, keys).astype(BF)
+    weight = (weight * keep[:, None, :]).reshape(rows, keys).astype(BF)
     value = jnp.concatenate([value, jnp.ones((keys, HD), BF)], axis=1)
     return jnp.dot(weight, value, preferred_element_type=F32)
 

time: 111 us -> 111 us (level)
  waiting for transfers between devices: 44.7 us -> 40.8 us
  starting transfers between devices: 51 us -> 54.8 us
    ppermute x10, waiting for transfers between devices: 28 us -> 25.5 us  [moved(): return lax.ppermute(x, ('dp', 'head'), pairs)]
    ppermute x10, starting transfers between devices: 19.5 us -> 21.4 us  [moved(): return lax.ppermute(x, ('dp', 'head'), pairs)]
    ppermute x9, waiting for transfers between devices: 1.92 us -> 0.02 us  [swapped(): return lax.ppermute(x, 'dp', [(0, 1), (1, 0)])]
    ppermute x9, starting transfers between devices: 8.16 us -> 10 us  [swapped(): return lax.ppermute(x, 'dp', [(0, 1), (1, 0)])]
  transfers between devices with their start and end apart: 35 -> 35, of which waited for: 18 -> 16; matrix products, arithmetic and copies ran while one was open for 0% -> 0% of each run, Pallas kernels for 10% -> 10%
where the time goes in v4:
time: 111 us
  starting transfers between devices  54.8 us (49%)
  waiting for transfers between devices  40.8 us (37%)
  Pallas kernels  12.9 us (12%)
  local copies, waits for them, and re-layouts  1.84 us (2%)
    ppermute x10, waiting for transfers between devices, moved(): return lax.ppermute(x, ('dp', 'head'), pairs)  25.5 us
    ppermute x10, starting transfers between devices, moved(): return lax.ppermute(x, ('dp', 'head'), pairs)  21.4 us
    ppermute x10, starting transfers between devices, along(): return lax.ppermute(x, axis, [(i, (i + step) % n) for i in range(n)])  13.1 us
    pallas_call x13, Pallas kernels, call(): pl.pallas_call(kernel, out_shape=out_shape, in_specs=[VMEM] * n, out_spec...  12.9 us
    ppermute x10, waiting for transfers between devices, along(): return lax.ppermute(x, axis, [(i, (i + step) % n) for i in range(n)])  11.5 us
    ppermute x6, starting transfers between devices, frames_on(): return lax.ppermute(x, ('dp', 'head'), pairs)  10.3 us
    ppermute x9, starting transfers between devices, swapped(): return lax.ppermute(x, 'dp', [(0, 1), (1, 0)])  10 us
    ppermute x6, waiting for transfers between devices, frames_on(): return lax.ppermute(x, ('dp', 'head'), pairs)  3.78 us
  transfers between devices with their start and end apart: 35, of which 16 were waited for; matrix products, arithmetic and copies ran while one was open for 0% of the time, Pallas kernels for 10%

profile of v4, /device:TPU:1, one launch (start us, length us, event | category | flops | bytes accessed | tf_op | source)
XLA Modules:
  0.0 110.6 jit_solution(4853521736777096193)
XLA Ops:
  0.0 3.3 %collective-permute-start.1 = (bf16[512,768]{1,0:T(8,128)(2,1)}, bf16[512,768]{1,0:T(8,128)(2,1)S(1)}, u32[]{:S(2)}, u32[]{:S(2)}) collective-permute-start(bf16[512,768]{1,0:T(8,128)(2,1)} %refs_0_.3), channel_id=1, source_target_pairs={{0,96},{32,0},{64,32},{96,64},{1,97},{33,1},{65,33},{97,65},{2,98}... | collective-permute-start | bytes 2359304 | tf_op jit(solution)/shard_map/ppermute | solution.py:47
  5.2 7.0 %collective-permute-start.4 = (bf16[192,384]{1,0:T(8,128)(2,1)S(1)}, bf16[192,384]{1,0:T(8,128)(2,1)S(1)}, u32[]{:S(2)}, u32[]{:S(2)}) collective-permute-start(bf16[192,384]{1,0:T(8,128)(2,1)S(1)} %prepare.1), channel_id=1, source_target_pairs={{0,2},{1,3},{2,0},{3,1},{4,6},{5,7},{6,4},{7,5},{8,10},{9,11},{10,... | collective-permute-start | bytes 442376 | tf_op jit(solution)/shard_map/ppermute | solution.py:33
  12.2 2.4 %collective-permute-start.2 = (bf16[192,384]{1,0:T(8,128)(2,1)S(1)}, bf16[192,384]{1,0:T(8,128)(2,1)S(1)}, u32[]{:S(2)}, u32[]{:S(2)}) collective-permute-start(bf16[192,384]{1,0:T(8,128)(2,1)S(1)} %prepare.1), channel_id=1, source_target_pairs={{0,1},{1,2},{2,3},{3,0},{4,5},{5,6},{6,7},{7,4},{8,9},{9,10},{10,1... | collective-permute-start | bytes 442376 | tf_op jit(solution)/shard_map/ppermute | solution.py:33
  14.8 5.4 %collective-permute-done.3 = bf16[192,384]{1,0:T(8,128)(2,1)S(1)} collective-permute-done((bf16[192,384]{1,0:T(8,128)(2,1)S(1)}, bf16[192,384]{1,0:T(8,128)(2,1)S(1)}, u32[]{:S(2)}, u32[]{:S(2)}) %collective-permute-start.3) | collective-permute-done | bytes 147488 | tf_op jit(solution)/shard_map/ppermute | solution.py:33
  20.3 2.5 %collective-permute-start.5 = (bf16[768,384]{1,0:T(8,128)(2,1)S(1)}, bf16[768,384]{1,0:T(8,128)(2,1)S(1)}, u32[]{:S(2)}, u32[]{:S(2)}) collective-permute-start(bf16[768,384]{1,0:T(8,128)(2,1)S(1)} %pad_maximum_fusion.refs_0_.refs_5_), channel_id=1, source_target_pairs={{0,4},{1,5},{2,6},{3,7},{4,8},{5,9},{6,10},{7,11},{8,12},{9,13},{1... | collective-permute-start | bytes 1769480 | tf_op jit(solution)/shard_map/ppermute | solution.py:33
  22.9 6.7 %collective-permute-done.5.refs_1_.refs_6_ = bf16[768,384]{1,0:T(8,128)(2,1)S(1)} collective-permute-done((bf16[768,384]{1,0:T(8,128)(2,1)S(1)}, bf16[768,384]{1,0:T(8,128)(2,1)S(1)}, u32[]{:S(2)}, u32[]{:S(2)}) %collective-permute-start.5) | collective-permute-done | bytes 589856 | tf_op jit(solution)/shard_map/ppermute | solution.py:33
  29.6 2.7 %collective-permute-start.6 = (bf16[768,384]{1,0:T(8,128)(2,1)S(1)}, bf16[768,384]{1,0:T(8,128)(2,1)S(1)}, u32[]{:S(2)}, u32[]{:S(2)}) collective-permute-start(bf16[768,384]{1,0:T(8,128)(2,1)S(1)} %pad_maximum_fusion.refs_0_.refs_5_), channel_id=1, source_target_pairs={{0,28},{1,29},{2,30},{3,31},{4,0},{5,1},{6,2},{7,3},{8,4},{9,5},{1... | collective-permute-start | bytes 1769480 | tf_op jit(solution)/shard_map/ppermute | solution.py:33
  32.3 2.7 %collective-permute-start.8 = (bf16[256,768]{1,0:T(8,128)(2,1)S(1)}, bf16[256,768]{1,0:T(8,128)(2,1)S(1)}, u32[]{:S(2)}, u32[]{:S(2)}) collective-permute-start(bf16[256,768]{1,0:T(8,128)(2,1)S(1)} %get-tuple-element.31), channel_id=1, source_target_pairs={{0,96},{32,0},{64,32},{96,64},{1,97},{33,1},{65,33},{97,65},{2,98}... | collective-permute-start | bytes 1179656 | tf_op jit(solution)/shard_map/ppermute | solution.py:47
  35.0 4.1 %collective-permute-done.6.refs_2_.refs_7_ = bf16[768,384]{1,0:T(8,128)(2,1)S(1)} collective-permute-done((bf16[768,384]{1,0:T(8,128)(2,1)S(1)}, bf16[768,384]{1,0:T(8,128)(2,1)S(1)}, u32[]{:S(2)}, u32[]{:S(2)}) %collective-permute-start.6) | collective-permute-done | bytes 589856 | tf_op jit(solution)/shard_map/ppermute | solution.py:33
  39.2 3.4 %collective-permute-start.10 = (bf16[768,384]{1,0:T(8,128)(2,1)S(1)}, bf16[768,384]{1,0:T(8,128)(2,1)S(1)}, u32[]{:S(2)}, u32[]{:S(2)}) collective-permute-start(bf16[768,384]{1,0:T(8,128)(2,1)S(1)} %collective-permute-done.6.refs_2_.refs_7_), channel_id=1, source_target_pairs={{0,28},{1,29},{2,30},{3,31},{4,0},{5,1},{6,2},{7,3},{8,4},{9,5},{1... | collective-permute-start | bytes 1769480 | tf_op jit(solution)/shard_map/ppermute | solution.py:33
  49.4 3.4 %collective-permute-start.14 = (bf16[768,384]{1,0:T(8,128)(2,1)S(1)}, bf16[768,384]{1,0:T(8,128)(2,1)S(1)}, u32[]{:S(2)}, u32[]{:S(2)}) collective-permute-start(bf16[768,384]{1,0:T(8,128)(2,1)S(1)} %collective-permute-done.10.refs_4_.refs_9_), channel_id=1, source_target_pairs={{0,28},{1,29},{2,30},{3,31},{4,0},{5,1},{6,2},{7,3},{8,4},{9,5},{1... | collective-permute-start | bytes 1769480 | tf_op jit(solution)/shard_map/ppermute | solution.py:33
  52.8 2.4 %collective-permute-start.18 = (bf16[512,768]{1,0:T(8,128)(2,1)S(1)}, bf16[512,768]{1,0:T(8,128)(2,1)S(1)}, u32[]{:S(2)}, u32[]{:S(2)}) collective-permute-start(bf16[512,768]{1,0:T(8,128)(2,1)S(1)} %copy-done), channel_id=1, source_target_pairs={{0,128},{128,0},{1,129},{129,1},{2,130},{130,2},{3,131},{131,3},{4... | collective-permute-start | bytes 2359304 | tf_op jit(solution)/shard_map/ppermute | solution.py:51
  55.7 3.9 %collective-permute-done.14.refs_6_.refs_11_ = bf16[768,384]{1,0:T(8,128)(2,1)S(1)} collective-permute-done((bf16[768,384]{1,0:T(8,128)(2,1)S(1)}, bf16[768,384]{1,0:T(8,128)(2,1)S(1)}, u32[]{:S(2)}, u32[]{:S(2)}) %collective-permute-start.14) | collective-permute-done | bytes 589856 | tf_op jit(solution)/shard_map/ppermute | solution.py:33
  59.6 3.4 %collective-permute-done.15.refs_7_.refs_12_ = bf16[768,384]{1,0:T(8,128)(2,1)S(1)} collective-permute-done((bf16[768,384]{1,0:T(8,128)(2,1)S(1)}, bf16[768,384]{1,0:T(8,128)(2,1)S(1)}, u32[]{:S(2)}, u32[]{:S(2)}) %collective-permute-start.15) | collective-permute-done | bytes 589856 | tf_op jit(solution)/shard_map/ppermute | solution.py:33
  63.2 3.0 %collective-permute-start.17 = (bf16[1536,384]{1,0:T(8,128)(2,1)S(1)}, bf16[1536,384]{1,0:T(8,128)(2,1)S(1)}, u32[]{:S(2)}, u32[]{:S(2)}) collective-permute-start(bf16[1536,384]{1,0:T(8,128)(2,1)S(1)} %query_half.1.w_own), channel_id=1, source_target_pairs={{0,128},{128,0},{1,129},{129,1},{2,130},{130,2},{3,131},{131,3},{4... | collective-permute-start | bytes 3538952 | tf_op jit(solution)/shard_map/ppermute | solution.py:51
  66.2 2.2 %project_cross.1 = (bf16[512,256]{1,0:T(8,128)(2,1)S(1)}, bf16[512,128]{1,0:T(8,128)(2,1)S(1)}, bf16[3072,384]{1,0:T(8,128)(2,1)S(1)}) custom-call(f32[2,128]{1,0:T(2,128)S(1)} %copy-done.1, bf16[512,768]{1,0:T(8,128)(2,1)S(1)} %collective-permute-done.18.refs_0_, bf16[512,768]{1,0:T(8,128)(2,1)S(1)} %collective-permute-done.19.refs_1_, ...), custom_call_target="tpu_custom_call" | custom-call | flops 1207959552 | bytes 6291456 | tf_op jit(solution)/shard_map/project_cross/pallas_call | solution.py:119
  73.1 3.7 %collective-permute-start.25 = (bf16[512,256]{1,0:T(8,128)(2,1)S(1)}, bf16[512,256]{1,0:T(8,128)(2,1)S(1)}, u32[]{:S(2)}, u32[]{:S(2)}) collective-permute-start(bf16[512,256]{1,0:T(8,128)(2,1)S(1)} %get-tuple-element.44.refs_0_), channel_id=1, source_target_pairs={{0,31},{1,0},{2,1},{3,2},{4,3},{5,4},{6,5},{7,6},{8,7},{9,8},{10,9... | collective-permute-start | bytes 786440 | tf_op jit(solution)/shard_map/ppermute | solution.py:42
  76.8 2.1 %query.1.q_ref = bf16[512,384]{1,0:T(8,128)(2,1)S(1)} custom-call(f32[2,128]{1,0:T(2,128)S(1)} %copy-done.1, bf16[1536,384]{1,0:T(8,128)(2,1)S(1)} %query_half.1.w_own, bf16[1536,384]{1,0:T(8,128)(2,1)S(1)} %collective-permute-done.17.w_other, bf16[512,768]{1,0:T(8,128)(2,1)S(1)} %copy-done, bf16[512,768]{1,0:T(8,128)(2,1)S(1)} %collective-permute-done.below.refs_1_, ...), custom_call_target="tpu_custom_call" | custom-call | flops 34359738368 | bytes 6291456 | tf_op jit(solution)/shard_map/query/pallas_call | solution.py:119
  79.0 4.9 %collective-permute-start.31 = (bf16[512,256]{1,0:T(8,128)(2,1)S(1)}, bf16[512,256]{1,0:T(8,128)(2,1)S(1)}, u32[]{:S(2)}, u32[]{:S(2)}) collective-permute-start(bf16[512,256]{1,0:T(8,128)(2,1)S(1)} %pack.1), channel_id=1, source_target_pairs={{0,31},{1,0},{2,1},{3,2},{4,3},{5,4},{6,5},{7,6},{8,7},{9,8},{10,9... | collective-permute-start | bytes 786440 | tf_op jit(solution)/shard_map/ppermute | solution.py:42
  85.0 2.2 %collective-permute-done.23.refs_0_ = bf16[512,256]{1,0:T(8,128)(2,1)S(1)} collective-permute-done((bf16[512,256]{1,0:T(8,128)(2,1)S(1)}, bf16[512,256]{1,0:T(8,128)(2,1)S(1)}, u32[]{:S(2)}, u32[]{:S(2)}) %collective-permute-start.23) | collective-permute-done | bytes 262176 | tf_op jit(solution)/shard_map/ppermute | solution.py:42
  88.6 2.0 %collective-permute-start.29 = (bf16[512,256]{1,0:T(8,128)(2,1)S(1)}, bf16[512,256]{1,0:T(8,128)(2,1)S(1)}, u32[]{:S(2)}, u32[]{:S(2)}) collective-permute-start(bf16[512,256]{1,0:T(8,128)(2,1)S(1)} %attend_0.1.refs_0_), channel_id=1, source_target_pairs={{0,64},{32,96},{64,0},{96,32},{1,65},{33,97},{65,1},{97,33},{2,66}... | collective-permute-start | bytes 786440 | tf_op jit(solution)/shard_map/ppermute | solution.py:47
  94.5 2.0 %collective-permute-start.34 = (bf16[512,128]{1,0:T(8,128)(2,1)S(1)}, bf16[512,128]{1,0:T(8,128)(2,1)S(1)}, u32[]{:S(2)}, u32[]{:S(2)}) collective-permute-start(bf16[512,128]{1,0:T(8,128)(2,1)S(1)} %attend_1.1.refs_0_), channel_id=1, source_target_pairs={{0,64},{32,96},{64,0},{96,32},{1,65},{33,97},{65,1},{97,33},{2,66}... | collective-permute-start | bytes 393224 | tf_op jit(solution)/shard_map/ppermute | solution.py:47
  98.1 5.9 %collective-permute-done.28.refs_2_ = bf16[512,256]{1,0:T(8,128)(2,1)S(1)} collective-permute-done((bf16[512,256]{1,0:T(8,128)(2,1)S(1)}, bf16[512,256]{1,0:T(8,128)(2,1)S(1)}, u32[]{:S(2)}, u32[]{:S(2)}) %collective-permute-start.28) | collective-permute-done | bytes 262176 | tf_op jit(solution)/shard_map/ppermute | solution.py:47
  106.0 2.6 %collective-permute-done.33.refs_2_ = bf16[512,128]{1,0:T(8,128)(2,1)S(1)} collective-permute-done((bf16[512,128]{1,0:T(8,128)(2,1)S(1)}, bf16[512,128]{1,0:T(8,128)(2,1)S(1)}, u32[]{:S(2)}, u32[]{:S(2)}) %collective-permute-start.33) | collective-permute-done | bytes 131104 | tf_op jit(solution)/shard_map/ppermute | solution.py:47
  (70 shorter events, 26.5 us)
Async XLA Ops:
  0.0 22.8 %collective-permute-start.1 = (bf16[512,768]{1,0:T(8,128)(2,1)}, bf16[512,768]{1,0:T(8,128)(2,1)S(1)}, u32[]{:S(2)}, u32[]{:S(2)}) collective-permute-start(bf16[512,768]{1,0:T(8,128)(2,1)} %refs_0_.3), channel_id=1, source_target_pairs={{0,96},{32,0},{64,32},{96,64},{1,97},{33,1},{65,33},{97,65},{2,98}... | collective-permute-start | bytes 2359304 | tf_op jit(solution)/shard_map/ppermute | solution.py:47
  3.3 19.5 %collective-permute-start = (bf16[512,768]{1,0:T(8,128)(2,1)}, bf16[512,768]{1,0:T(8,128)(2,1)S(1)}, u32[]{:S(2)}, u32[]{:S(2)}) collective-permute-start(bf16[512,768]{1,0:T(8,128)(2,1)} %refs_0_.3), channel_id=1, source_target_pairs={{0,32},{32,64},{64,96},{96,0},{1,33},{33,65},{65,97},{97,1},{2,34}... | collective-permute-start | bytes 2359304 | tf_op jit(solution)/shard_map/ppermute | solution.py:47
  32.3 10.2 %collective-permute-start.7 = (bf16[768,384]{1,0:T(8,128)(2,1)S(1)}, bf16[768,384]{1,0:T(8,128)(2,1)S(1)}, u32[]{:S(2)}, u32[]{:S(2)}) collective-permute-start(bf16[768,384]{1,0:T(8,128)(2,1)S(1)} %collective-permute-done.5.refs_1_.refs_6_), channel_id=1, source_target_pairs={{0,4},{1,5},{2,6},{3,7},{4,8},{5,9},{6,10},{7,11},{8,12},{9,13},{1... | collective-permute-start | bytes 1769480 | tf_op jit(solution)/shard_map/ppermute | solution.py:33
  32.3 10.5 %collective-permute-start.8 = (bf16[256,768]{1,0:T(8,128)(2,1)S(1)}, bf16[256,768]{1,0:T(8,128)(2,1)S(1)}, u32[]{:S(2)}, u32[]{:S(2)}) collective-permute-start(bf16[256,768]{1,0:T(8,128)(2,1)S(1)} %get-tuple-element.31), channel_id=1, source_target_pairs={{0,96},{32,0},{64,32},{96,64},{1,97},{33,1},{65,33},{97,65},{2,98}... | collective-permute-start | bytes 1179656 | tf_op jit(solution)/shard_map/ppermute | solution.py:47
  35.0 10.9 %collective-permute-start.11 = (bf16[256,768]{1,0:T(8,128)(2,1)S(1)}, bf16[256,768]{1,0:T(8,128)(2,1)S(1)}, u32[]{:S(2)}, u32[]{:S(2)}) collective-permute-start(bf16[256,768]{1,0:T(8,128)(2,1)S(1)} %get-tuple-element.33), channel_id=1, source_target_pairs={{0,32},{32,64},{64,96},{96,0},{1,33},{33,65},{65,97},{97,1},{2,34}... | collective-permute-start | bytes 1179656 | tf_op jit(solution)/shard_map/ppermute | solution.py:47
  39.2 10.2 %collective-permute-start.10 = (bf16[768,384]{1,0:T(8,128)(2,1)S(1)}, bf16[768,384]{1,0:T(8,128)(2,1)S(1)}, u32[]{:S(2)}, u32[]{:S(2)}) collective-permute-start(bf16[768,384]{1,0:T(8,128)(2,1)S(1)} %collective-permute-done.6.refs_2_.refs_7_), channel_id=1, source_target_pairs={{0,28},{1,29},{2,30},{3,31},{4,0},{5,1},{6,2},{7,3},{8,4},{9,5},{1... | collective-permute-start | bytes 1769480 | tf_op jit(solution)/shard_map/ppermute | solution.py:33
  42.6 10.2 %collective-permute-start.13 = (bf16[768,384]{1,0:T(8,128)(2,1)S(1)}, bf16[768,384]{1,0:T(8,128)(2,1)S(1)}, u32[]{:S(2)}, u32[]{:S(2)}) collective-permute-start(bf16[768,384]{1,0:T(8,128)(2,1)S(1)} %collective-permute-done.7.refs_3_.refs_8_), channel_id=1, source_target_pairs={{0,4},{1,5},{2,6},{3,7},{4,8},{5,9},{6,10},{7,11},{8,12},{9,13},{1... | collective-permute-start | bytes 1769480 | tf_op jit(solution)/shard_map/ppermute | solution.py:33
  49.4 10.2 %collective-permute-start.14 = (bf16[768,384]{1,0:T(8,128)(2,1)S(1)}, bf16[768,384]{1,0:T(8,128)(2,1)S(1)}, u32[]{:S(2)}, u32[]{:S(2)}) collective-permute-start(bf16[768,384]{1,0:T(8,128)(2,1)S(1)} %collective-permute-done.10.refs_4_.refs_9_), channel_id=1, source_target_pairs={{0,28},{1,29},{2,30},{3,31},{4,0},{5,1},{6,2},{7,3},{8,4},{9,5},{1... | collective-permute-start | bytes 1769480 | tf_op jit(solution)/shard_map/ppermute | solution.py:33
  52.8 10.2 %collective-permute-start.15 = (bf16[768,384]{1,0:T(8,128)(2,1)S(1)}, bf16[768,384]{1,0:T(8,128)(2,1)S(1)}, u32[]{:S(2)}, u32[]{:S(2)}) collective-permute-start(bf16[768,384]{1,0:T(8,128)(2,1)S(1)} %collective-permute-done.13.refs_5_.refs_10_), channel_id=1, source_target_pairs={{0,4},{1,5},{2,6},{3,7},{4,8},{5,9},{6,10},{7,11},{8,12},{9,13},{1... | collective-permute-start | bytes 1769480 | tf_op jit(solution)/shard_map/ppermute | solution.py:33
  52.8 13.4 %collective-permute-start.18 = (bf16[512,768]{1,0:T(8,128)(2,1)S(1)}, bf16[512,768]{1,0:T(8,128)(2,1)S(1)}, u32[]{:S(2)}, u32[]{:S(2)}) collective-permute-start(bf16[512,768]{1,0:T(8,128)(2,1)S(1)} %copy-done), channel_id=1, source_target_pairs={{0,128},{128,0},{1,129},{129,1},{2,130},{130,2},{3,131},{131,3},{4... | collective-permute-start | bytes 2359304 | tf_op jit(solution)/shard_map/ppermute | solution.py:51
  55.2 11.0 %collective-permute-start.19 = (bf16[512,768]{1,0:T(8,128)(2,1)S(1)}, bf16[512,768]{1,0:T(8,128)(2,1)S(1)}, u32[]{:S(2)}, u32[]{:S(2)}) collective-permute-start(bf16[512,768]{1,0:T(8,128)(2,1)S(1)} %collective-permute-done.below.refs_1_), channel_id=1, source_target_pairs={{0,128},{128,0},{1,129},{129,1},{2,130},{130,2},{3,131},{131,3},{4... | collective-permute-start | bytes 2359304 | tf_op jit(solution)/shard_map/ppermute | solution.py:51
  55.3 10.9 %collective-permute-start.20 = (bf16[512,768]{1,0:T(8,128)(2,1)S(1)}, bf16[512,768]{1,0:T(8,128)(2,1)S(1)}, u32[]{:S(2)}, u32[]{:S(2)}) collective-permute-start(bf16[512,768]{1,0:T(8,128)(2,1)S(1)} %collective-permute-done.1.above.refs_2_), channel_id=1, source_target_pairs={{0,128},{128,0},{1,129},{129,1},{2,130},{130,2},{3,131},{131,3},{4... | collective-permute-start | bytes 2359304 | tf_op jit(solution)/shard_map/ppermute | solution.py:51
  63.2 13.6 %collective-permute-start.17 = (bf16[1536,384]{1,0:T(8,128)(2,1)S(1)}, bf16[1536,384]{1,0:T(8,128)(2,1)S(1)}, u32[]{:S(2)}, u32[]{:S(2)}) collective-permute-start(bf16[1536,384]{1,0:T(8,128)(2,1)S(1)} %query_half.1.w_own), channel_id=1, source_target_pairs={{0,128},{128,0},{1,129},{129,1},{2,130},{130,2},{3,131},{131,3},{4... | collective-permute-start | bytes 3538952 | tf_op jit(solution)/shard_map/ppermute | solution.py:51
  69.1 9.9 %collective-permute-start.26 = (bf16[512,256]{1,0:T(8,128)(2,1)S(1)}, bf16[512,256]{1,0:T(8,128)(2,1)S(1)}, u32[]{:S(2)}, u32[]{:S(2)}) collective-permute-start(bf16[512,256]{1,0:T(8,128)(2,1)S(1)} %get-tuple-element.40), channel_id=1, source_target_pairs={{0,159},{1,128},{2,129},{3,130},{4,131},{5,132},{6,133},{7,134},{8... | collective-permute-start | bytes 786440 | tf_op jit(solution)/shard_map/ppermute | solution.py:42
  69.3 14.5 %collective-permute-start.24 = (bf16[512,256]{1,0:T(8,128)(2,1)S(1)}, bf16[512,256]{1,0:T(8,128)(2,1)S(1)}, u32[]{:S(2)}, u32[]{:S(2)}) collective-permute-start(bf16[512,256]{1,0:T(8,128)(2,1)S(1)} %get-tuple-element.40), channel_id=1, source_target_pairs={{0,129},{1,130},{2,131},{3,132},{4,133},{5,134},{6,135},{7,136},{8... | collective-permute-start | bytes 786440 | tf_op jit(solution)/shard_map/ppermute | solution.py:42
  71.0 25.5 %collective-permute-start.16 = (bf16[1536,384]{1,0:T(8,128)(2,1)S(1)}, bf16[1536,384]{1,0:T(8,128)(2,1)S(1)}, u32[]{:S(2)}, u32[]{:S(2)}) collective-permute-start(bf16[1536,384]{1,0:T(8,128)(2,1)S(1)} %out_half.1.w_own), channel_id=1, source_target_pairs={{0,128},{128,0},{1,129},{129,1},{2,130},{130,2},{3,131},{131,3},{4... | collective-permute-start | bytes 3538952 | tf_op jit(solution)/shard_map/ppermute | solution.py:51
  73.1 11.9 %collective-permute-start.25 = (bf16[512,256]{1,0:T(8,128)(2,1)S(1)}, bf16[512,256]{1,0:T(8,128)(2,1)S(1)}, u32[]{:S(2)}, u32[]{:S(2)}) collective-permute-start(bf16[512,256]{1,0:T(8,128)(2,1)S(1)} %get-tuple-element.44.refs_0_), channel_id=1, source_target_pairs={{0,31},{1,0},{2,1},{3,2},{4,3},{5,4},{6,5},{7,6},{8,7},{9,8},{10,9... | collective-permute-start | bytes 786440 | tf_op jit(solution)/shard_map/ppermute | solution.py:42
  76.8 10.5 %collective-permute-start.23 = (bf16[512,256]{1,0:T(8,128)(2,1)S(1)}, bf16[512,256]{1,0:T(8,128)(2,1)S(1)}, u32[]{:S(2)}, u32[]{:S(2)}) collective-permute-start(bf16[512,256]{1,0:T(8,128)(2,1)S(1)} %get-tuple-element.44.refs_0_), channel_id=1, source_target_pairs={{0,1},{1,2},{2,3},{3,4},{4,5},{5,6},{6,7},{7,8},{8,9},{9,10},{10,1... | collective-permute-start | bytes 786440 | tf_op jit(solution)/shard_map/ppermute | solution.py:42
  79.0 12.7 %collective-permute-start.31 = (bf16[512,256]{1,0:T(8,128)(2,1)S(1)}, bf16[512,256]{1,0:T(8,128)(2,1)S(1)}, u32[]{:S(2)}, u32[]{:S(2)}) collective-permute-start(bf16[512,256]{1,0:T(8,128)(2,1)S(1)} %pack.1), channel_id=1, source_target_pairs={{0,31},{1,0},{2,1},{3,2},{4,3},{5,4},{6,5},{7,6},{8,7},{9,8},{10,9... | collective-permute-start | bytes 786440 | tf_op jit(solution)/shard_map/ppermute | solution.py:42
  90.6 13.4 %collective-permute-start.28 = (bf16[512,256]{1,0:T(8,128)(2,1)S(1)}, bf16[512,256]{1,0:T(8,128)(2,1)S(1)}, u32[]{:S(2)}, u32[]{:S(2)}) collective-permute-start(bf16[512,256]{1,0:T(8,128)(2,1)S(1)} %attend_0.1.refs_0_), channel_id=1, source_target_pairs={{0,96},{32,0},{64,32},{96,64},{1,97},{33,1},{65,33},{97,65},{2,98}... | collective-permute-start | bytes 786440 | tf_op jit(solution)/shard_map/ppermute | solution.py:47
  91.7 13.0 %collective-permute-start.27 = (bf16[512,256]{1,0:T(8,128)(2,1)S(1)}, bf16[512,256]{1,0:T(8,128)(2,1)S(1)}, u32[]{:S(2)}, u32[]{:S(2)}) collective-permute-start(bf16[512,256]{1,0:T(8,128)(2,1)S(1)} %attend_0.1.refs_0_), channel_id=1, source_target_pairs={{0,32},{32,64},{64,96},{96,0},{1,33},{33,65},{65,97},{97,1},{2,34}... | collective-permute-start | bytes 786440 | tf_op jit(solution)/shard_map/ppermute | solution.py:47
  94.5 11.4 %collective-permute-start.34 = (bf16[512,128]{1,0:T(8,128)(2,1)S(1)}, bf16[512,128]{1,0:T(8,128)(2,1)S(1)}, u32[]{:S(2)}, u32[]{:S(2)}) collective-permute-start(bf16[512,128]{1,0:T(8,128)(2,1)S(1)} %attend_1.1.refs_0_), channel_id=1, source_target_pairs={{0,64},{32,96},{64,0},{96,32},{1,65},{33,97},{65,1},{97,33},{2,66}... | collective-permute-start | bytes 393224 | tf_op jit(solution)/shard_map/ppermute | solution.py:47
  96.5 12.1 %collective-permute-start.33 = (bf16[512,128]{1,0:T(8,128)(2,1)S(1)}, bf16[512,128]{1,0:T(8,128)(2,1)S(1)}, u32[]{:S(2)}, u32[]{:S(2)}) collective-permute-start(bf16[512,128]{1,0:T(8,128)(2,1)S(1)} %attend_1.1.refs_0_), channel_id=1, source_target_pairs={{0,96},{32,0},{64,32},{96,64},{1,97},{33,1},{65,33},{97,65},{2,98}... | collective-permute-start | bytes 393224 | tf_op jit(solution)/shard_map/ppermute | solution.py:47
  97.6 11.4 %collective-permute-start.32 = (bf16[512,128]{1,0:T(8,128)(2,1)S(1)}, bf16[512,128]{1,0:T(8,128)(2,1)S(1)}, u32[]{:S(2)}, u32[]{:S(2)}) collective-permute-start(bf16[512,128]{1,0:T(8,128)(2,1)S(1)} %attend_1.1.refs_0_), channel_id=1, source_target_pairs={{0,32},{32,64},{64,96},{96,0},{1,33},{33,65},{65,97},{97,1},{2,34}... | collective-permute-start | bytes 393224 | tf_op jit(solution)/shard_map/ppermute | solution.py:47
  (16 other events, 162.1 us)
